TPU v7x, 32 devices: a whole 2x2x4 slice. The times are simulated.
32 devices in a mesh: ctx: 8 (over y, x, core), fsdp: 4 (over z).
Axes of the slice: x: 2, y: 2, z: 4, core: 2. Of those that a mesh axis runs over, the one named last changes fastest.
Arguments:
- hidden_states: bfloat16 [8, 2048, 768], P('fsdp', 'ctx'), may hold values from -6 to 6
- lengths: int32 [8], P('fsdp'), may hold values from 128 to 2048, as said below
- cotangent: bfloat16 [8, 2048, 768], P('fsdp', 'ctx'), may hold values from -6 to 6
- attend_weight: bfloat16 [768, 2304], P('fsdp'), may hold values from -0.21875 to 0.21875
- query_bias: bfloat16 [768], P('fsdp'), may hold values from -3 to 3
- value_bias: bfloat16 [768], P('fsdp'), may hold values from -0.119628906 to 0.119628906
- output_weight: bfloat16 [768, 768], P('fsdp'), may hold values from -3.5 to 3.5
- output_bias: bfloat16 [768], P('fsdp'), may hold values from -3 to 3
- first_gain: bfloat16 [768], P('fsdp'), may hold values from 0.099609375 to 1.8984375
- first_shift: bfloat16 [768], P('fsdp'), may hold values from -3 to 3
- raise_weight: bfloat16 [768, 3072], P('fsdp'), may hold values from -0.21875 to 0.21875
- raise_bias: bfloat16 [3072], P('fsdp'), may hold values from -3 to 3
- lower_weight: bfloat16 [3072, 768], P('fsdp'), may hold values from -0.109375 to 0.109375
- lower_bias: bfloat16 [768], P('fsdp'), may hold values from -3 to 3
- second_gain: bfloat16 [768], P('fsdp'), may hold values from 0.099609375 to 1.8984375
- second_shift: bfloat16 [768], P('fsdp'), may hold values from -3 to 3
Outputs:
- layer_output: bfloat16 [8, 2048, 768], P('fsdp', 'ctx')
- hidden_grad: float32 [8, 2048, 768], P('fsdp', 'ctx')
- grad_attend_weight: float32 [768, 2304], P('fsdp')
- grad_query_bias: float32 [768], P('fsdp')
- grad_value_bias: float32 [768], P('fsdp')
- grad_output_weight: float32 [768, 768], P('fsdp')
- grad_output_bias: float32 [768], P('fsdp')
- grad_first_gain: float32 [768], P('fsdp')
- grad_first_shift: float32 [768], P('fsdp')
- grad_raise_weight: float32 [768, 3072], P('fsdp')
- grad_raise_bias: float32 [3072], P('fsdp')
- grad_lower_weight: float32 [3072, 768], P('fsdp')
- grad_lower_bias: float32 [768], P('fsdp')
- grad_second_gain: float32 [768], P('fsdp')
- grad_second_shift: float32 [768], P('fsdp')
Inputs may be any that keep to these rules, and one draw needn't show every extreme that they name: `lengths`: among the 2 sequences of each index of fsdp, one drawn from the seed has length exactly 2048; the others are drawn evenly.
All inputs are finite; a program needn't handle non-finite values.
Results may differ from a plain program's by a relative error of at most 0.02.
Values may be sent and summed in bfloat16 or wider, within the bound.
No kernel may reach another device: no remote copies, remote signals or barrier semaphores. Data moves between devices by JAX's collectives and lax.ppermute only.
A program may use at most 320 MiB of HBM per device.

v0:
```python
import math

import jax
import jax.numpy as jnp
from jax import lax
from jax.sharding import PartitionSpec as P

HEADS = 12
HEAD_DIM = 64


def layer_norm(hidden, gain, shift):
    average = jnp.mean(hidden, axis=-1, keepdims=True)
    centred = hidden - average
    variance = jnp.mean(centred * centred, axis=-1, keepdims=True)
    return centred * lax.rsqrt(variance + 1e-05) * gain + shift


def gelu_exact(inputs):
    return jax.nn.gelu(inputs, approximate=False)


def split_heads(blocked):
    return blocked.reshape(blocked.shape[0], blocked.shape[1], HEADS, HEAD_DIM)


def merge_heads(per_head, row_count, model_width):
    return jnp.swapaxes(per_head, 1, 2).reshape(row_count, model_width)


def by_sequence(compute, running, seq_count):
    return compute(running, slice(0, seq_count))


def on_device(
    hidden_states,
    lengths,
    cotangent,
    attend_weight,
    query_bias,
    value_bias,
    output_weight,
    output_bias,
    first_gain,
    first_shift,
    raise_weight,
    raise_bias,
    lower_weight,
    lower_bias,
    second_gain,
    second_shift,
):
    seq_count, tok_count, model_width = hidden_states.shape
    row_count = seq_count * tok_count
    scale_factor = 1.0 / math.sqrt(HEAD_DIM)
    gathered = (
        lax.all_gather(attend_weight, "fsdp", axis=0, tiled=True),
        lax.all_gather(output_weight, "fsdp", axis=0, tiled=True),
        lax.all_gather(raise_weight, "fsdp", axis=0, tiled=True),
        lax.all_gather(lower_weight, "fsdp", axis=0, tiled=True),
        lax.all_gather(query_bias, "fsdp", axis=0, tiled=True),
        lax.all_gather(value_bias, "fsdp", axis=0, tiled=True),
        lax.all_gather(output_bias, "fsdp", axis=0, tiled=True),
        lax.all_gather(first_gain, "fsdp", axis=0, tiled=True),
        lax.all_gather(first_shift, "fsdp", axis=0, tiled=True),
        lax.all_gather(raise_bias, "fsdp", axis=0, tiled=True),
        lax.all_gather(lower_bias, "fsdp", axis=0, tiled=True),
        lax.all_gather(second_gain, "fsdp", axis=0, tiled=True),
        lax.all_gather(second_shift, "fsdp", axis=0, tiled=True),
    )
    attend_full, output_full, raise_full, lower_full = (
        gathered[0],
        gathered[1],
        gathered[2],
        gathered[3],
    )
    (
        query_add,
        value_add,
        output_add,
        gain_first,
        shift_first,
        raise_add,
        lower_add,
        gain_second,
        shift_second,
    ) = [vector.astype(jnp.float32) for vector in gathered[4:]]
    token_rows = hidden_states.reshape(row_count, model_width)
    mixture = jnp.dot(token_rows, attend_full, preferred_element_type=jnp.float32)
    block_shape = (seq_count, tok_count, model_width)
    queries = (mixture[:, :model_width] + query_add).astype(jnp.bfloat16).reshape(block_shape)
    keys_here = mixture[:, model_width : 2 * model_width].astype(jnp.bfloat16).reshape(block_shape)
    values_here = (
        (mixture[:, 2 * model_width :] + value_add).astype(jnp.bfloat16).reshape(block_shape)
    )
    query_heads = split_heads(queries)
    key_heads_here = split_heads(keys_here)
    value_heads_here = split_heads(values_here)
    own_offset = lax.axis_index("ctx") * tok_count

    def allowed_keys(offset, number):
        places = offset + jnp.arange(number, dtype=jnp.int32)
        return (places[None, :] < lengths[:, None])[:, None, None, :]

    stat_shape = (seq_count, HEADS, tok_count)
    initial = (
        jnp.full(stat_shape, -1000000000.0, jnp.float32),
        jnp.zeros(stat_shape, jnp.float32),
        jnp.zeros(stat_shape + (HEAD_DIM,), jnp.float32),
    )
    pieces = (
        lax.all_gather(keys_here, "ctx", axis=1, tiled=True),
        lax.all_gather(values_here, "ctx", axis=1, tiled=True),
    )
    offset = jnp.int32(0)

    def compute(state, picked):
        highest, summed, weighted = state
        key_part = split_heads(pieces[0])
        value_part = split_heads(pieces[1])
        allowed = allowed_keys(offset, pieces[0].shape[1])
        scores = (
            jnp.einsum("sqhd,skhd->shqk", query_heads, key_part, preferred_element_type=jnp.float32)
            * scale_factor
        )
        scores = jnp.where(allowed, scores, -1000000000.0)
        new_high = jnp.maximum(highest, jnp.max(scores, axis=-1))
        weights = jnp.exp(scores - new_high[..., None]) * allowed
        summed = jnp.sum(weights, axis=-1)
        weighted = jnp.einsum(
            "shqk,skhd->shqd",
            weights.astype(jnp.bfloat16),
            value_part,
            preferred_element_type=jnp.float32,
        )
        return (new_high, summed, weighted)

    highest, summed, weighted = by_sequence(compute, initial, seq_count)
    attended_heads = weighted / summed[..., None]
    log_total = highest + jnp.log(summed)
    attended_low = merge_heads(attended_heads, row_count, model_width).astype(jnp.bfloat16)
    projected = jnp.dot(attended_low, output_full, preferred_element_type=jnp.float32) + output_add
    normed_first, first_back = jax.vjp(
        layer_norm, token_rows.astype(jnp.float32) + projected, gain_first, shift_first
    )
    first_low = normed_first.astype(jnp.bfloat16)
    raised = jnp.dot(first_low, raise_full, preferred_element_type=jnp.float32) + raise_add
    active, gelu_back = jax.vjp(gelu_exact, raised)
    active_low = active.astype(jnp.bfloat16)
    lowered = jnp.dot(active_low, lower_full, preferred_element_type=jnp.float32) + lower_add
    result, second_back = jax.vjp(layer_norm, normed_first + lowered, gain_second, shift_second)
    layer_output = result.astype(jnp.bfloat16).reshape(block_shape)
    grad_out = cotangent.reshape(row_count, model_width).astype(jnp.float32)
    grad_mid, grad_gain_second, grad_shift_second = second_back(grad_out)
    mid_low = grad_mid.astype(jnp.bfloat16)
    grad_lower_weight = jnp.einsum(
        "rf,rd->fd", active_low, mid_low, preferred_element_type=jnp.float32
    )
    grad_lower_add = jnp.sum(mid_low.astype(jnp.float32), axis=0)
    grad_active = jnp.einsum("rd,fd->rf", mid_low, lower_full, preferred_element_type=jnp.float32)
    (grad_raised,) = gelu_back(grad_active)
    raised_low = grad_raised.astype(jnp.bfloat16)
    grad_raise_weight = jnp.einsum(
        "rd,rf->df", first_low, raised_low, preferred_element_type=jnp.float32
    )
    grad_raise_add = jnp.sum(raised_low.astype(jnp.float32), axis=0)
    grad_first = grad_mid + jnp.einsum(
        "rf,df->rd", raised_low, raise_full, preferred_element_type=jnp.float32
    )
    grad_resid, grad_gain_first, grad_shift_first = first_back(grad_first)
    resid_low = grad_resid.astype(jnp.bfloat16)
    grad_output_weight = jnp.einsum(
        "rc,rd->cd", attended_low, resid_low, preferred_element_type=jnp.float32
    )
    grad_output_add = jnp.sum(resid_low.astype(jnp.float32), axis=0)
    grad_att = (
        jnp.einsum("rd,cd->rc", resid_low, output_full, preferred_element_type=jnp.float32)
        .astype(jnp.bfloat16)
        .reshape(block_shape)
    )
    grad_heads = split_heads(grad_att)
    delta = jnp.einsum("sthd,shtd->sht", grad_heads.astype(jnp.float32), attended_heads)
    head_zeros = jnp.zeros(stat_shape + (HEAD_DIM,), jnp.float32)
    all_lse, all_delta = (
        lax.all_gather(log_total, "ctx", axis=2, tiled=True),
        lax.all_gather(delta, "ctx", axis=2, tiled=True),
    )
    key_pieces = (
        lax.all_gather(queries, "ctx", axis=1, tiled=True),
        lax.all_gather(grad_att, "ctx", axis=1, tiled=True),
    )

    def compute(state, picked):
        query_part = split_heads(key_pieces[0])
        grad_part = split_heads(key_pieces[1])
        number = key_pieces[0].shape[1]
        own_allowed = allowed_keys(own_offset, tok_count)
        scores = (
            jnp.einsum(
                "sqhd,skhd->shqk", query_part, key_heads_here, preferred_element_type=jnp.float32
            )
            * scale_factor
        )
        scores = jnp.where(own_allowed, scores, -1000000000.0)
        weights = jnp.exp(scores - all_lse[..., None]) * own_allowed
        grad_values = jnp.einsum(
            "shqk,sqhd->shkd",
            weights.astype(jnp.bfloat16),
            grad_part,
            preferred_element_type=jnp.float32,
        )
        grad_weights = jnp.einsum(
            "sqhd,skhd->shqk", grad_part, value_heads_here, preferred_element_type=jnp.float32
        )
        grad_scores = (weights * (grad_weights - all_delta[..., None])).astype(jnp.bfloat16)
        grad_keys = (
            jnp.einsum(
                "shqk,sqhd->shkd", grad_scores, query_part, preferred_element_type=jnp.float32
            )
            * scale_factor
        )
        return (grad_keys, grad_values)

    grad_keys, grad_values = by_sequence(compute, (head_zeros, head_zeros), seq_count)
    query_pieces = (
        lax.all_gather(keys_here, "ctx", axis=1, tiled=True),
        lax.all_gather(values_here, "ctx", axis=1, tiled=True),
    )
    query_offset = jnp.int32(0)

    def compute(state, picked):
        key_part = split_heads(query_pieces[0])
        value_part = split_heads(query_pieces[1])
        allowed = allowed_keys(query_offset, query_pieces[0].shape[1])
        scores = (
            jnp.einsum("sqhd,skhd->shqk", query_heads, key_part, preferred_element_type=jnp.float32)
            * scale_factor
        )
        scores = jnp.where(allowed, scores, -1000000000.0)
        weights = jnp.exp(scores - log_total[..., None]) * allowed
        grad_weights = jnp.einsum(
            "sqhd,skhd->shqk", grad_heads, value_part, preferred_element_type=jnp.float32
        )
        grad_scores = (weights * (grad_weights - delta[..., None])).astype(jnp.bfloat16)
        return (
            jnp.einsum("shqk,skhd->shqd", grad_scores, key_part, preferred_element_type=jnp.float32)
            * scale_factor
        )

    grad_queries = by_sequence(compute, head_zeros, seq_count)
    query_low = merge_heads(grad_queries, row_count, model_width).astype(jnp.bfloat16)
    key_low = merge_heads(grad_keys, row_count, model_width).astype(jnp.bfloat16)
    value_low = merge_heads(grad_values, row_count, model_width).astype(jnp.bfloat16)
    grad_mixture = jnp.concatenate([query_low, key_low, value_low], axis=1)
    grad_attend_weight = jnp.einsum(
        "rd,rc->dc", token_rows, grad_mixture, preferred_element_type=jnp.float32
    )
    grad_query_add = jnp.sum(query_low.astype(jnp.float32), axis=0)
    grad_value_add = jnp.sum(value_low.astype(jnp.float32), axis=0)
    hidden_grad = grad_resid + jnp.einsum(
        "rc,dc->rd", grad_mixture, attend_full, preferred_element_type=jnp.float32
    )
    summed_all = lax.psum(
        (
            grad_attend_weight,
            grad_query_add,
            grad_value_add,
            grad_output_weight,
            grad_output_add,
            grad_gain_first,
            grad_shift_first,
            grad_raise_weight,
            grad_raise_add,
            grad_lower_weight,
            grad_lower_add,
            grad_gain_second,
            grad_shift_second,
        ),
        "ctx",
    )
    owned = (
        lax.psum_scatter(summed_all[0], "fsdp", scatter_dimension=0, tiled=True),
        lax.psum_scatter(summed_all[1], "fsdp", scatter_dimension=0, tiled=True),
        lax.psum_scatter(summed_all[2], "fsdp", scatter_dimension=0, tiled=True),
        lax.psum_scatter(summed_all[3], "fsdp", scatter_dimension=0, tiled=True),
        lax.psum_scatter(summed_all[4], "fsdp", scatter_dimension=0, tiled=True),
        lax.psum_scatter(summed_all[5], "fsdp", scatter_dimension=0, tiled=True),
        lax.psum_scatter(summed_all[6], "fsdp", scatter_dimension=0, tiled=True),
        lax.psum_scatter(summed_all[7], "fsdp", scatter_dimension=0, tiled=True),
        lax.psum_scatter(summed_all[8], "fsdp", scatter_dimension=0, tiled=True),
        lax.psum_scatter(summed_all[9], "fsdp", scatter_dimension=0, tiled=True),
        lax.psum_scatter(summed_all[10], "fsdp", scatter_dimension=0, tiled=True),
        lax.psum_scatter(summed_all[11], "fsdp", scatter_dimension=0, tiled=True),
        lax.psum_scatter(summed_all[12], "fsdp", scatter_dimension=0, tiled=True),
    )
    return (
        layer_output,
        hidden_grad.reshape(block_shape),
        owned[0],
        owned[1],
        owned[2],
        owned[3],
        owned[4],
        owned[5],
        owned[6],
        owned[7],
        owned[8],
        owned[9],
        owned[10],
        owned[11],
        owned[12],
    )


def solution(mesh):
    return jax.shard_map(
        on_device,
        mesh=mesh,
        in_specs=(
            P("fsdp", "ctx", None),
            P("fsdp"),
            P("fsdp", "ctx", None),
            P("fsdp", None),
            P("fsdp"),
            P("fsdp"),
            P("fsdp", None),
            P("fsdp"),
            P("fsdp"),
            P("fsdp"),
            P("fsdp", None),
            P("fsdp"),
            P("fsdp", None),
            P("fsdp"),
            P("fsdp"),
            P("fsdp"),
        ),
        out_specs=(
            P("fsdp", "ctx", None),
            P("fsdp", "ctx", None),
            P("fsdp", None),
            P("fsdp"),
            P("fsdp"),
            P("fsdp", None),
            P("fsdp"),
            P("fsdp"),
            P("fsdp"),
            P("fsdp", None),
            P("fsdp"),
            P("fsdp", None),
            P("fsdp"),
            P("fsdp"),
            P("fsdp"),
        ),
        check_vma=False,
    )
```

profile of v0, /device:TPU:0, one launch (start us, length us, event | category | flops | bytes accessed | tf_op | source)
XLA Modules:
  0.0 1228.3 jit_solution(4885120821952417126)
XLA Ops:
  8.0 74.3 %all-gather.10.cloned.1.call-done = bf16[768,2304]{1,0:T(8,128)(2,1)} async-done(((bf16[192,2304]{1,0:T(8,128)(2,1)}), bf16[768,2304]{1,0:T(8,128)(2,1)}) %all-gather.10.cloned.1.call-update) | async-done | bytes 3538960 | tf_op jit(solution)/shard_map/all_gather | solution.py:57
  93.1 16.1 %all-reduce.20 = (bf16[768]{0:T(1024)(128)(2,1)S(1)}, bf16[768]{0:T(1024)(128)(2,1)S(1)}, bf16[768]{0:T(1024)(128)(2,1)S(1)}, bf16[768]{0:T(1024)(128)(2,1)S(1)}...) all-reduce(bf16[768]{0:T(1024)(128)(2,1)S(1)} %dynamic-update-slice, ...), channel_id=1, replica_groups=mesh['ctx'=8,'fsdp'=4] {'fsdp'}, use_global_device_ids=true, to_apply=%add.1 | all-reduce | flops 6144 | bytes 24576
  114.1 13.0 %all-gather = bf16[4,1,768]{2,1,0:T(2,128)(2,1)S(1)} all-gather(bf16[1,1,768]{2,1,0:T(2,128)(2,1)S(1)} %reshape.275), channel_id=1, replica_groups=mesh['ctx'=8,'fsdp'=4] {'fsdp'}, dimensions={0}, use_global_device_ids=true | all-gather | bytes 7680 | tf_op jit(solution)/shard_map/all_gather | solution.py:66
  128.1 6.2 all-gather.12.cloned.1.call-done
  134.3 8.7 copy.54
  143.0 23.9 %fusion.3 = (f32[2,12,256]{2,1,0:T(8,128)S(1)}, f32[2,12,256,2048]{3,2,1,0:T(8,128)}) fusion(pred[2,2048]{1,0:T(4,128)(4,1)S(1)} %get-tuple-element.114, bf16[2,2048,12,64]{1,3,2,0:T(8,128)(2,1)} %bitcast.104, bf16[2,256,12,64]{1,0,3,2:T(2,128)(2,1)S(1)} %reshape_reshape.12), kind=kOutput, calls=%fused_computation.8 | convolution fusion | flops 1648355328 | bytes 57438208 | tf_op jit(solution)/shard_map/sqhd,skhd->shqk/dot_general | solution.py:123
  166.9 22.2 %fusion = f32[2,12,256]{2,1,0:T(8,128)S(1)} fusion(f32[2,12,256,2048]{3,2,1,0:T(8,128)} %get-tuple-element.117, f32[2,2048]{1,0:T(2,128)S(1)} %get-tuple-element.115, f32[2,12,256]{2,1,0:T(8,128)S(1)} %broadcast_maximum_fusion, pred[2,2048]{1,0:T(4,128)(4,1)S(1)} %get-tuple-element.114), kind=kLoop, calls=%fused_computation.5 | loop fusion | flops 62908416 | bytes 50401280 | tf_op jit(solution)/shard_map/reduce_sum | solution.py:129
  189.1 8.8 copy.56
  197.9 22.7 %fusion.30 = (bf16[2,256,12,64]{1,3,2,0:T(8,128)(2,1)S(1)}, f32[2,12,256,64]{2,3,1,0:T(8,128)}) fusion(f32[2,256,12]{1,2,0:T(8,128)S(1)} %bitcast.131, bf16[2,2048,12,64]{1,3,2,0:T(8,128)(2,1)} %bitcast.111, f32[2,12,256,2048]{3,2,1,0:T(8,128)} %get-tuple-element.117, f32[2,2048]{1,0:T(2,128)S(1)} %get-tuple-element.115, ...), kind=kOutput, calls=%fused_computation.53 | convolution fusion | flops 1674313728 | bytes 59052032 | tf_op jit(solution)/shard_map/shqk,skhd->shqd/dot_general | solution.py:130
  224.5 79.1 %all-gather.18.cloned.1.call-done = bf16[768,3072]{1,0:T(8,128)(2,1)} async-done(((bf16[192,3072]{1,0:T(8,128)(2,1)}), bf16[768,3072]{1,0:T(8,128)(2,1)}) %all-gather.18.cloned.1.call-update) | async-done | bytes 4718608 | tf_op jit(solution)/shard_map/all_gather | solution.py:59
  303.6 20.0 %multiply_convert_fusion.4 = (bf16[512,3072]{1,0:T(8,128)(2,1)}, f32[512,3072]{1,0:T(8,128)}, f32[512,3072]{1,0:T(8,128)}) fusion(f32[3072]{0:T(1024)S(1)} %bitcast.132, bf16[768,3072]{1,0:T(8,128)(2,1)} %all-gather.18.cloned.1.call-done, f32[512,768]{1,0:T(8,128)S(1)} %get-tuple-element.121, f32[768]{0:T(1024)S(1)} %convert_element_type.164, ...), kind=kOutput, calls=%fused_computation.23 | convolution fusion | flops 2521694208 | bytes 22042624 | tf_op jit(solution)/shard_map/dot_general | solution.py:147
  323.6 69.3 %all-gather.20.cloned.1.call-done = bf16[3072,768]{1,0:T(8,128)(2,1)} async-done(((bf16[768,768]{1,0:T(8,128)(2,1)}), bf16[3072,768]{1,0:T(8,128)(2,1)}) %all-gather.20.cloned.1.call-update) | async-done | bytes 4718608 | tf_op jit(solution)/shard_map/all_gather | solution.py:60
  392.9 6.2 fusion.65
  403.2 9.0 convert_reduce_fusion
  429.1 28.3 %convert_reduce_fusion.5 = (f32[12,64]{1,0:T(8,128)S(1)}, bf16[2,12,256,64]{2,3,1,0:T(8,128)(2,1)S(1)}) fusion(bf16[2,2048,12,64]{1,3,2,0:T(8,128)(2,1)} %bitcast.105, f32[2,12,256,2048]{3,2,1,0:T(8,128)} %get-tuple-element.117, f32[2,12,256]{2,1,0:T(8,128)S(1)} %multiply_reduce_fusion, f32[2,12,256]{2,1,0:T(8,128)S(1)} %log_add_fusion, ...), kind=kOutput, calls=%fused_computation.59 | convolution fusion | flops 3310877952 | bytes 64560128 | tf_op jit(solution)/shard_map/shqk,skhd->shqd/dot_general | solution.py:246
  459.3 9.0 copy.61
  468.3 10.3 all_gather.77
  478.5 10.5 all_gather.75
  490.2 20.7 %fusion.38 = f32[2,12,2048,256]{3,2,1,0:T(8,128)} fusion(bf16[2,2048,12,64]{1,3,2,0:T(8,128)(2,1)} %bitcast.106, bf16[2,256,12,64]{1,0,3,2:T(2,128)(2,1)S(1)} %reshape_reshape.14), kind=kOutput, calls=%fused_computation.79 | convolution fusion | flops 1610612736 | bytes 57409536 | tf_op jit(solution)/shard_map/sqhd,skhd->shqk/dot_general | solution.py:199
  511.0 8.6 copy.64
  519.6 21.2 %convert_reduce_fusion.4 = (f32[12,64]{1,0:T(8,128)S(1)}, bf16[2,12,256,64]{2,3,1,0:T(8,128)(2,1)}) fusion(bf16[2,2048,12,64]{1,3,2,0:T(8,128)(2,1)} %bitcast.113, f32[2,12,2048,256]{3,2,1,0:T(8,128)} %fusion.38, f32[2,256]{1,0:T(2,128)S(1)} %get-tuple-element.101, f32[2,12,2048]{2,1,0:T(8,128)} %all_gather.75, pred[2,256]{1,0:T(4,128)(4,1)S(1)} %get-tuple-element.102), kind=kOutput, calls=%fused_computation.58 | convolution fusion | flops 1674706176 | bytes 57611776 | tf_op jit(solution)/shard_map/shqk,sqhd->shkd/dot_general | solution.py:206
  540.8 27.6 %fusion.34 = bf16[2,256,12,64]{1,3,2,0:T(8,128)(2,1)} fusion(bf16[2,2048,12,64]{1,3,2,0:T(8,128)(2,1)} %bitcast.107, f32[2,12,2048,256]{3,2,1,0:T(8,128)} %fusion.38, f32[2,12,2048]{2,1,0:T(8,128)S(1)} %all_gather.77, f32[2,256]{1,0:T(2,128)S(1)} %get-tuple-element.101, f32[2,12,2048]{2,1,0:T(8,128)} %all_gather.75, ...), kind=kOutput, calls=%fused_computation.75 | convolution fusion | flops 3310092288 | bytes 64883200 | tf_op jit(solution)/shard_map/shqk,sqhd->shkd/dot_general | solution.py:217
  577.8 8.0 copy.75
  589.5 8.2 fusion.55
  598.8 8.1 fusion.70
  607.1 100.5 %reduce-scatter.13.cloned.1.call-done = f32[192,2304]{1,0:T(8,128)} async-done(((f32[768,2304]{1,0:T(8,128)}), f32[192,2304]{1,0:T(8,128)}) %reduce-scatter.13.cloned.1.call-update) | async-done | bytes 1769488
  710.6 47.8 %reduce-scatter.7.cloned.1.call-done = f32[192,768]{1,0:T(8,128)} async-done(((f32[768,768]{1,0:T(8,128)}), f32[192,768]{1,0:T(8,128)}) %reduce-scatter.7.cloned.1.call-update) | async-done | bytes 589840 | tf_op jit(solution)/shard_map/reduce_scatter | solution.py:285
  758.4 163.2 %reduce-scatter.9.cloned.1.call-done = f32[192,3072]{1,0:T(8,128)} async-done(((f32[768,3072]{1,0:T(8,128)}), f32[192,3072]{1,0:T(8,128)}) %reduce-scatter.9.cloned.1.call-update) | async-done | bytes 2359312 | tf_op jit(solution)/shard_map/reduce_scatter | solution.py:289
  921.6 164.4 %reduce-scatter.11.cloned.1.call-done = f32[768,768]{1,0:T(8,128)} async-done(((f32[3072,768]{1,0:T(8,128)}), f32[768,768]{1,0:T(8,128)}) %reduce-scatter.11.cloned.1.call-update) | async-done | bytes 2359312 | tf_op jit(solution)/shard_map/reduce_scatter | solution.py:291
  1087.6 19.0 %all-reduce.19 = (f32[768]{0:T(1024)S(1)}, f32[768]{0:T(1024)S(1)}, f32[768]{0:T(1024)S(1)}, f32[768]{0:T(1024)S(1)}, f32[768]{0:T(1024)S(1)}, /*index=5*/f32[30...) all-reduce(f32[768]{0:T(1024)S(1)} %reduce_sum.208, ...), channel_id=3, replica_groups=mesh['ctx'=8,'fsdp'=4] {'fsdp'}, use_global_device_ids=true, to_apply=%region_14.15.clone | all-reduce | flops 9216 | bytes 73728
  1107.2 24.4 %all-reduce.17 = (f32[192]{0:T(256)}, f32[192]{0:T(256)}, f32[192]{0:T(256)}, f32[192]{0:T(256)}, f32[192]{0:T(256)}, /*index=5*/f32[768]{0:T(1024)}, f32[192]{0:T(256)}, f32[192]{0:T(256)}, f32[192]{0:T(256)}) all-reduce(f32[192]{0:T(256)S(1)} %dynamic-slice.9, ...), channel_id=1, replica_groups=mesh['ctx'=8,'fsdp'=4] {'ctx'}, use_global_device_ids=true, to_apply=%region_13.14 | all-reduce | flops 2304 | bytes 18432 | tf_op jit(solution)/shard_map/psum | solution.py:263
  1137.6 74.0 %all-reduce.23.cloned.1.call-done = (f32[192,2304]{0,1:T(8,128)}, f32[192,768]{1,0:T(8,128)}, f32[192,3072]{1,0:T(8,128)}, f32[768,768]{1,0:T(8,128)}) async-done(((f32[192,2304]{0,1:T(8,128)}, f32[192,768]{1,0:T(8,128)}, f32[192,3072]{1,0:T(8,128)}, f32[768,768]{1,0:T(8,128)}), (f32[192,2304]{0,1:T(8,128)}, f32[192,768]{1,0:T(8,128)}, f32[192,3072]{1,0:T(8,128)}, ...) | async-done | bytes 7077904 | tf_op jit(solution)/shard_map/psum | solution.py:263
  (238 shorter events, 77.8 us)
Async XLA Ops:
  7.2 75.1 %all-gather.10.cloned.1.call-start = ((), (), s32[]{:S(2)}) async-start(), calls=%async_computation.4 | async-start | bytes 4423680 | tf_op jit(solution)/shard_map/all_gather | solution.py:57
  7.9 126.4 %all-gather.12.cloned.1.call-start = ((), (), s32[]{:S(2)}) async-start(), calls=%async_computation.5 | async-start | bytes 7077888 | tf_op jit(solution)/shard_map/all_gather | solution.py:112
  88.9 25.1 %copy-start.41 = (bf16[768]{0:T(1024)(128)(2,1)S(1)}, bf16[768]{0:T(1024)(128)(2,1)}, u32[]{:S(2)}) copy-start(bf16[768]{0:T(1024)(128)(2,1)} %param.27) | copy-start | bytes 4612
  89.0 38.3 %copy-start.38 = (s32[2]{0:T(128)S(1)}, s32[2]{0:T(128)}, u32[]{:S(2)}) copy-start(s32[2]{0:T(128)} %param.17) | copy-start | bytes 28
  89.9 99.2 %all-gather.14.cloned.1.call-start = ((), (), s32[]{:S(2)}) async-start(), calls=%async_computation.6 | async-start | bytes 7077888 | tf_op jit(solution)/shard_map/all_gather | solution.py:113
  112.2 109.3 %all-gather.16.cloned.1.call-start = ((), (), s32[]{:S(2)}) async-start(), calls=%async_computation.7 | async-start | bytes 1474560 | tf_op jit(solution)/shard_map/all_gather | solution.py:58
  112.8 190.8 %all-gather.18.cloned.1.call-start = ((), (), s32[]{:S(2)}) async-start(), calls=%async_computation.8 | async-start | bytes 5898240 | tf_op jit(solution)/shard_map/all_gather | solution.py:59
  113.4 279.5 %all-gather.20.cloned.1.call-start = ((), (), s32[]{:S(2)}) async-start(), calls=%async_computation.9 | async-start | bytes 5898240 | tf_op jit(solution)/shard_map/all_gather | solution.py:60
  114.0 345.3 %all-gather.22.cloned.1.call-start = ((), (), s32[]{:S(2)}) async-start(), calls=%async_computation.10 | async-start | bytes 7077888 | tf_op jit(solution)/shard_map/all_gather | solution.py:189
  127.2 265.8 %copy-start.34 = (f32[768]{0:T(1024)}, f32[768]{0:T(1024)S(1)}, u32[]{:S(2)}) copy-start(f32[768]{0:T(1024)S(1)} %convert_element_type.164) | copy-start | bytes 9220
  127.2 288.7 %copy-start.27 = (f32[768]{0:T(1024)}, f32[768]{0:T(1024)S(1)}, u32[]{:S(2)}) copy-start(f32[768]{0:T(1024)S(1)} %convert_element_type.163) | copy-start | bytes 9220
  127.8 383.2 %all-gather.24.cloned.1.call-start = ((), (), s32[]{:S(2)}) async-start(), calls=%async_computation.11 | async-start | bytes 7077888 | tf_op jit(solution)/shard_map/all_gather | solution.py:190
  197.9 23.7 %copy-start.20 = (bf16[2,256,768]{2,1,0:T(8,128)(2,1)S(1)}, bf16[2,256,768]{2,1,0:T(8,128)(2,1)}, u32[]{:S(2)}) copy-start(bf16[2,256,768]{2,1,0:T(8,128)(2,1)} %param.16) | copy-start | bytes 2359300
  221.5 102.1 %copy-start.12 = (bf16[96,8,2,256]{3,1,2,0:T(8,128)(2,1)}, bf16[96,8,2,256]{3,1,2,0:T(8,128)(2,1)S(1)}, u32[]{:S(2)}) copy-start(bf16[96,8,2,256]{3,1,2,0:T(8,128)(2,1)S(1)} %copy.77) | copy-start | bytes 2359300
  224.2 191.7 %copy-start.5 = (f32[512,768]{1,0:T(8,128)}, f32[512,768]{1,0:T(8,128)S(1)}, u32[]{:S(2)}) copy-start(f32[512,768]{1,0:T(8,128)S(1)} %get-tuple-element.121) | copy-start | bytes 4718596
  224.2 191.7 %copy-start.22 = (f32[512]{0:T(512)}, f32[512]{0:T(512)S(1)}, u32[]{:S(2)}) copy-start(f32[512]{0:T(512)S(1)} %broadcast_multiply_fusion.1) | copy-start | bytes 6148
  224.5 191.4 %copy-start.30 = (f32[512]{0:T(512)}, f32[512]{0:T(512)S(1)}, u32[]{:S(2)}) copy-start(f32[512]{0:T(512)S(1)} %fusion.44) | copy-start | bytes 6148
  421.1 286.5 %reduce-scatter.13.cloned.1.call-start = ((), (), s32[]{:S(2)}) async-start(), calls=%async_computation.15 | async-start | bytes 8847360
  519.6 21.2 %copy-start.17 = (bf16[2,256,12,64]{1,0,3,2:T(2,128)(2,1)S(1)}, bf16[2,256,12,64]{1,0,3,2:T(2,128)(2,1)}, u32[]{:S(2)}) copy-start(bf16[2,256,12,64]{1,0,3,2:T(2,128)(2,1)} %reshape_reshape.15) | copy-start | bytes 2359300
  585.9 172.5 %reduce-scatter.7.cloned.1.call-start = ((), (), s32[]{:S(2)}) async-start(), calls=%async_computation.12 | async-start | bytes 2949120 | tf_op jit(solution)/shard_map/reduce_scatter | solution.py:285
  589.4 332.2 %reduce-scatter.9.cloned.1.call-start = ((), (), s32[]{:S(2)}) async-start(), calls=%async_computation.13 | async-start | bytes 11796480 | tf_op jit(solution)/shard_map/reduce_scatter | solution.py:289
  597.7 488.3 %reduce-scatter.11.cloned.1.call-start = ((), (), s32[]{:S(2)}) async-start(), calls=%async_computation.14 | async-start | bytes 11796480 | tf_op jit(solution)/shard_map/reduce_scatter | solution.py:291
  607.0 480.3 %copy-start.1 = (bf16[2,256,768]{2,1,0:T(8,128)(2,1)S(1)}, bf16[2,256,768]{2,1,0:T(8,128)(2,1)}, u32[]{:S(2)}) copy-start(bf16[2,256,768]{2,1,0:T(8,128)(2,1)} %param.18) | copy-start | bytes 2359300
  607.0 480.6 %copy-start.24 = (f32[768]{0:T(1024)S(1)}, f32[768]{0:T(1024)}, u32[]{:S(2)}) copy-start(f32[768]{0:T(1024)} %get-tuple-element.62) | copy-start | bytes 9220
  607.0 480.6 %copy-start.25 = (f32[768]{0:T(1024)S(1)}, f32[768]{0:T(1024)}, u32[]{:S(2)}) copy-start(f32[768]{0:T(1024)} %get-tuple-element.95) | copy-start | bytes 9220
  607.0 480.6 %copy-start.26 = (f32[768]{0:T(1024)S(1)}, f32[768]{0:T(1024)}, u32[]{:S(2)}) copy-start(f32[768]{0:T(1024)} %get-tuple-element.99) | copy-start | bytes 9220
  607.0 480.6 %copy-start.29 = (f32[3072]{0:T(1024)S(1)}, f32[3072]{0:T(1024)}, u32[]{:S(2)}) copy-start(f32[3072]{0:T(1024)} %get-tuple-element.97) | copy-start | bytes 36868
  607.0 480.6 %copy-start.36 = (f32[768]{0:T(1024)S(1)}, f32[768]{0:T(1024)}, u32[]{:S(2)}) copy-start(f32[768]{0:T(1024)} %get-tuple-element.60) | copy-start | bytes 9220
  607.0 480.6 %copy-start.37 = (f32[768]{0:T(1024)S(1)}, f32[768]{0:T(1024)}, u32[]{:S(2)}) copy-start(f32[768]{0:T(1024)} %get-tuple-element.64) | copy-start | bytes 9220
  607.0 524.6 %copy-start.8 = (f32[512,768]{1,0:T(8,128)S(1)}, f32[512,768]{1,0:T(8,128)}, u32[]{:S(2)}) copy-start(f32[512,768]{1,0:T(8,128)} %copy-done.7) | copy-start | bytes 4718596
  607.0 524.6 %copy-start.33 = (f32[512]{0:T(512)S(1)}, f32[512]{0:T(512)}, u32[]{:S(2)}) copy-start(f32[512]{0:T(512)} %copy-done.32) | copy-start | bytes 6148
  607.0 604.5 %all-reduce.23.cloned.1.call-start = ((), (), s32[]{:S(2)}) async-start(), calls=%async_computation.16 | async-start | bytes 15335424 | tf_op jit(solution)/shard_map/psum | solution.py:263
  (37 other events, 246.9 us)
Sparse Core Ops, SparseCore 0:
  9.6 72.6 all-gather.9
  90.1 44.1 all-gather.11
  136.2 45.5 all-gather.13
  183.2 30.4 all-gather.15
  215.0 88.5 all-gather.17
  305.0 87.8 all-gather.19
  394.8 43.9 all-gather.21
  440.7 46.9 all-gather.23
  586.0 121.5 reduce-scatter.12
  709.8 48.5 reduce-scatter.6
  760.7 160.7 reduce-scatter.8
  923.8 162.1 reduce-scatter.10
  1090.2 121.3 all-reduce.22
where the time goes:
time: 1230 us
  waiting for transfers between devices  781 us (63%)
  matrix products  221 us (18%)
  blocking collectives  93.3 us (8%)
  local copies, waits for them, and re-layouts  81 us (7%)
  other arithmetic  33.7 us (3%)
  between operations  17.2 us (1%)
    reduce_scatter x1, waiting for transfers between devices, on_device(): lax.psum_scatter(summed_all[9], 'fsdp', scatter_dimension=0, tiled=True)  164 us
    reduce_scatter x1, waiting for transfers between devices, on_device(): lax.psum_scatter(summed_all[7], 'fsdp', scatter_dimension=0, tiled=True)  163 us
    unnamed x14, waiting for transfers between devices  103 us
    all_gather x1, waiting for transfers between devices, on_device(): lax.all_gather(raise_weight, 'fsdp', axis=0, tiled=True)  79.1 us
    all_gather x1, waiting for transfers between devices, on_device(): lax.all_gather(attend_weight, 'fsdp', axis=0, tiled=True)  74.3 us
    psum x1, waiting for transfers between devices, on_device(): lax.psum((grad_attend_weight, grad_query_add, grad_value_add, grad_output...  74 us
    all_gather x1, waiting for transfers between devices, on_device(): lax.all_gather(lower_weight, 'fsdp', axis=0, tiled=True)  69.3 us
    reduce_scatter x1, waiting for transfers between devices, on_device(): lax.psum_scatter(summed_all[3], 'fsdp', scatter_dimension=0, tiled=True)  47.8 us
  transfers between devices with their start and end apart: 13, of which 9 were waited for; matrix products, arithmetic and copies ran while one was open for 19% of the time, Pallas kernels for 0%

commit v1 on v0

v1 whole, which is shorter than its diff:
```python
import functools
import math

import jax
import jax.numpy as jnp
from jax import lax
from jax.experimental import pallas as pl
from jax.experimental.pallas import tpu as pltpu
from jax.sharding import PartitionSpec as P

HEADS = 12
HEAD_DIM = 64
PAIR = 2 * HEAD_DIM
LOG2E = 1.4426950408889634
SCORE = LOG2E / math.sqrt(HEAD_DIM)
F32 = jnp.float32
BF16 = jnp.bfloat16
CHUNK_BLOCKS = 2
NT = (((1,), (1,)), ((), ()))


def layer_norm(hidden, gain, shift):
    average = jnp.mean(hidden, axis=-1, keepdims=True)
    centred = hidden - average
    variance = jnp.mean(centred * centred, axis=-1, keepdims=True)
    return centred * lax.rsqrt(variance + 1e-05) * gain + shift


def gelu_exact(inputs):
    return jax.nn.gelu(inputs, approximate=False)


def swap(value, bit):
    number = lax.axis_size("ctx")
    return lax.ppermute(value, "ctx", [(at, at ^ bit) for at in range(number)])


def shift_fsdp(value, step):
    number = lax.axis_size("fsdp")
    return lax.ppermute(value, "fsdp", [(at, (at + step) % number) for at in range(number)])


def ctx_bits():
    bits, bit = [], 2
    while bit < lax.axis_size("ctx"):
        bits.append(bit)
        bit *= 2
    return bits


def gather_ctx(piece, order):
    me = lax.axis_index("ctx")
    held, done = piece, []
    for bit in order:
        other = swap(held, bit)
        high = (me & bit) != 0
        place = sum(1 for earlier in done if earlier > bit)
        held = jnp.stack([jnp.where(high, other, held), jnp.where(high, held, other)], axis=place)
        done.append(bit)
    return held.reshape((lax.axis_size("ctx"),) + piece.shape)


def scatter_ctx_step(held, bits_left, bit):
    me = lax.axis_index("ctx")
    high = (me & bit) // bit
    axis = 1 + bits_left.index(bit)
    mine = lax.dynamic_index_in_dim(held, high, axis, keepdims=False)
    send = lax.dynamic_index_in_dim(held, 1 - high, axis, keepdims=False).astype(BF16)
    total = mine.astype(F32) + swap(send, bit).astype(F32)
    return total.astype(BF16), [left for left in bits_left if left != bit]


def sum_weight(partial):
    rows, columns = partial.shape
    number, groups = lax.axis_size("ctx"), lax.axis_size("fsdp")
    own = lax.axis_index("fsdp")
    chips = ctx_bits()
    all_bits = sorted(chips + [1], reverse=True)
    held = partial.reshape((groups,) + (2,) * len(all_bits) + (rows // (groups * number), columns))
    held, left = scatter_ctx_step(held, all_bits, 1)
    half = columns // 2
    pieces = []
    for part, order in ((held[..., :half], chips), (held[..., half:], chips[::-1])):
        part_left = left
        for bit in order:
            part, part_left = scatter_ctx_step(part, part_left, bit)
        pieces.append(part)
    piece = jnp.concatenate(pieces, axis=-1)
    total = lax.dynamic_index_in_dim(piece, own, 0, keepdims=False).astype(F32)
    for step in range(1, groups):
        send = lax.dynamic_index_in_dim(piece, (own + step) % groups, 0, keepdims=False)
        total = total + shift_fsdp(send, step).astype(F32)
    total = total.astype(BF16)
    left_half = gather_ctx(total[:, :half], chips[::-1] + [1])
    right_half = gather_ctx(total[:, half:], chips + [1])
    whole = jnp.concatenate([left_half, right_half], axis=-1)
    return whole.reshape(rows // groups, columns).astype(F32)


def sum_vectors(vectors):
    groups = lax.axis_size("fsdp")
    own = lax.axis_index("fsdp")
    packed = jnp.concatenate([vector.reshape(groups, -1) for vector in vectors], axis=1)
    for bit in [1] + ctx_bits():
        packed = packed + swap(packed, bit)
    total = lax.dynamic_index_in_dim(packed, own, 0, keepdims=False)
    for step in range(1, groups):
        send = lax.dynamic_index_in_dim(packed, (own + step) % groups, 0, keepdims=False)
        total = total + shift_fsdp(send, step)
    owned, at = [], 0
    for vector in vectors:
        width = vector.shape[0] // groups
        owned.append(total[at : at + width])
        at += width
    return owned


def gather_vectors(vectors):
    groups = lax.axis_size("fsdp")
    own = lax.axis_index("fsdp")
    packed = jnp.concatenate(vectors)[None]
    whole = jnp.zeros((groups, packed.shape[1]), packed.dtype)
    whole = lax.dynamic_update_slice(whole, packed, (own, 0))
    for step in range(1, groups):
        other = shift_fsdp(packed, step)
        whole = lax.dynamic_update_slice(whole, other, ((own - step) % groups, 0))
    gathered, at = [], 0
    for vector in vectors:
        width = vector.shape[0]
        gathered.append(whole[:, at : at + width].reshape(-1).astype(F32))
        at += width
    return gathered


def gather_weight_core(shard):
    rows, columns = shard.shape
    groups = lax.axis_size("fsdp")
    own = lax.axis_index("fsdp")
    core = lax.axis_index("ctx") % 2
    halves = shard.reshape(2, rows // 2, columns)
    whole = jnp.zeros((groups, 2, rows // 2, columns), shard.dtype)
    whole = lax.dynamic_update_slice(whole, halves[None], (own, 0, 0, 0))
    piece = lax.dynamic_index_in_dim(halves, core, 0, keepdims=False)
    for step in range(1, groups):
        piece = shift_fsdp(piece, 1)
        at = (own - step) % groups
        whole = lax.dynamic_update_slice(whole, piece[None, None], (at, core, 0, 0))
        whole = lax.dynamic_update_slice(whole, swap(piece, 1)[None, None], (at, 1 - core, 0, 0))
    return whole.reshape(groups * rows, columns)


def gather_weight_ctx(shard):
    rows, columns = shard.shape
    number, groups = lax.axis_size("ctx"), lax.axis_size("fsdp")
    own, me = lax.axis_index("fsdp"), lax.axis_index("ctx")
    chips = ctx_bits()
    half = columns // 2
    parts = shard.reshape(number, rows // number, columns)
    whole = jnp.zeros((groups, number, rows // number, columns), shard.dtype)
    whole = lax.dynamic_update_slice(whole, parts[None], (own, 0, 0, 0))
    piece = lax.dynamic_index_in_dim(parts, me, 0, keepdims=False)
    for step in range(1, groups):
        piece = shift_fsdp(piece, 1)
        at = (own - step) % groups
        left_half = gather_ctx(piece[:, :half], chips + [1])
        right_half = gather_ctx(piece[:, half:], chips[::-1] + [1])
        whole = lax.dynamic_update_slice(whole, left_half[None], (at, 0, 0, 0))
        whole = lax.dynamic_update_slice(whole, right_half[None], (at, 0, 0, half))
    return whole.reshape(groups * rows, columns)


def head_masks(rows):
    lane = lax.broadcasted_iota(jnp.int32, (rows, PAIR), 1)
    first = lane < HEAD_DIM
    return (first, jnp.logical_not(first))


def of_head(pair, mask):
    return jnp.where(mask, pair.astype(F32), 0.0).astype(BF16)


def lane_fold(values, combine):
    width = values.shape[1]
    folded = values[:, :PAIR]
    for at in range(PAIR, width, PAIR):
        folded = combine(folded, values[:, at : at + PAIR])
    return folded


def chunk_of(ref, index):
    part = ref[pl.ds(index * CHUNK_BLOCKS, CHUNK_BLOCKS)]
    return part.reshape(part.shape[0] * part.shape[1], PAIR)


def key_bias(length, index, width):
    place = index * width + lax.broadcasted_iota(jnp.int32, (1, width), 1)
    return jnp.where(place < length, 0.0, -1e30)


def forward_kernel(place_ref, q_ref, k_ref, v_ref, att_ref, low_ref, col_ref, row_ref, scores):
    length = place_ref[1]
    rows = q_ref.shape[1]
    width = CHUNK_BLOCKS * k_ref.shape[1]
    chunks = (length + width - 1) // width
    masks = head_masks(rows)
    queries = q_ref[0]
    split = [of_head(queries, mask) for mask in masks]

    def score_chunk(index, tops):
        keys = chunk_of(k_ref, index)
        bias = key_bias(length, index, width)
        new = []
        for head in range(2):
            part = lax.dot_general(split[head], keys, NT, preferred_element_type=F32) + bias
            scores[head, index] = part
            new.append(jnp.maximum(tops[head], lane_fold(part, jnp.maximum)))
        return tuple(new)

    low_start = jnp.full((rows, PAIR), -1e30, F32)
    tops = lax.fori_loop(0, chunks, score_chunk, (low_start, low_start))
    top = [jnp.max(one, axis=1, keepdims=True) * SCORE for one in tops]

    def weigh_chunk(index, state):
        values = chunk_of(v_ref, index)
        new = []
        for head in range(2):
            summed, weighted = state[head]
            weights = jnp.exp2(scores[head, index] * SCORE - top[head])
            summed = summed + lane_fold(weights, jnp.add)
            weighted = weighted + jnp.dot(
                weights.astype(BF16), values, preferred_element_type=F32
            )
            new.append((summed, weighted))
        return tuple(new)

    zero = jnp.zeros((rows, PAIR), F32)
    state = lax.fori_loop(0, chunks, weigh_chunk, ((zero, zero), (zero, zero)))
    totals = [jnp.sum(state[head][0], axis=1, keepdims=True) for head in range(2)]
    attended = jnp.where(masks[0], state[0][1] / totals[0], state[1][1] / totals[1])
    att_ref[...] = attended
    low_ref[...] = attended.astype(BF16)
    lse = [top[head] + jnp.log2(totals[head]) for head in range(2)]
    column = jnp.where(masks[0], lse[0], lse[1])
    col_ref[...] = column
    turned = jnp.transpose(column)
    row_ref[0, 0:1, :] = turned[0:1, :]
    row_ref[0, 1:2, :] = turned[HEAD_DIM : HEAD_DIM + 1, :]


def query_kernel(place_ref, q_ref, k_ref, v_ref, g_ref, att_ref, col_ref, out_ref):
    length = place_ref[1]
    rows = q_ref.shape[1]
    width = CHUNK_BLOCKS * k_ref.shape[1]
    chunks = (length + width - 1) // width
    masks = head_masks(rows)
    grads = g_ref[...]
    products = grads.astype(F32) * att_ref[...]
    query_split = [of_head(q_ref[0], mask) for mask in masks]
    grad_split = [of_head(grads, mask) for mask in masks]
    delta = [jnp.sum(jnp.where(mask, products, 0.0), axis=1, keepdims=True) for mask in masks]
    lse = [col_ref[:, 0:1], col_ref[:, HEAD_DIM : HEAD_DIM + 1]]

    def chunk(index, totals):
        keys = chunk_of(k_ref, index)
        values = chunk_of(v_ref, index)
        bias = key_bias(length, index, width)
        new = []
        for head in range(2):
            part = lax.dot_general(query_split[head], keys, NT, preferred_element_type=F32)
            weights = jnp.exp2(part * SCORE - lse[head] + bias)
            moved = lax.dot_general(grad_split[head], values, NT, preferred_element_type=F32)
            grad_scores = (weights * (moved - delta[head])).astype(BF16)
            new.append(totals[head] + jnp.dot(grad_scores, keys, preferred_element_type=F32))
        return tuple(new)

    zero = jnp.zeros((rows, PAIR), F32)
    totals = lax.fori_loop(0, chunks, chunk, (zero, zero))
    total = jnp.where(masks[0], totals[0], totals[1])
    out_ref[...] = (total * (1.0 / math.sqrt(HEAD_DIM))).astype(BF16)


def key_kernel(place_ref, k_ref, v_ref, q_ref, g_ref, stat_ref, dk_ref, dv_ref):
    offset, length = place_ref[0] * k_ref.shape[1], place_ref[1]
    rows = k_ref.shape[1]
    chunks = q_ref.shape[0] // CHUNK_BLOCKS
    masks = head_masks(rows)

    @pl.when(offset >= length)
    def _():
        dk_ref[...] = jnp.zeros(dk_ref.shape, BF16)
        dv_ref[...] = jnp.zeros(dv_ref.shape, BF16)

    @pl.when(offset < length)
    def _():
        key_split = [of_head(k_ref[0], mask) for mask in masks]
        value_split = [of_head(v_ref[0], mask) for mask in masks]

        def chunk(index, totals):
            queries = chunk_of(q_ref, index)
            grads = chunk_of(g_ref, index)
            stats = stat_ref[pl.ds(index * CHUNK_BLOCKS, CHUNK_BLOCKS), 0]

            def stat(which):
                return jnp.concatenate(
                    [stats[at, which : which + 1, :] for at in range(CHUNK_BLOCKS)], axis=1
                )

            new = []
            for head in range(2):
                part = lax.dot_general(key_split[head], queries, NT, preferred_element_type=F32)
                weights = jnp.exp2(part * SCORE - stat(head))
                moved = lax.dot_general(value_split[head], grads, NT, preferred_element_type=F32)
                grad_scores = (weights * (moved - stat(2 + head))).astype(BF16)
                grad_keys, grad_values = totals[head]
                grad_keys = grad_keys + jnp.dot(grad_scores, queries, preferred_element_type=F32)
                grad_values = grad_values + jnp.dot(
                    weights.astype(BF16), grads, preferred_element_type=F32
                )
                new.append((grad_keys, grad_values))
            return tuple(new)

        zero = jnp.zeros((rows, PAIR), F32)
        totals = lax.fori_loop(0, chunks, chunk, ((zero, zero), (zero, zero)))
        usable = offset + lax.broadcasted_iota(jnp.int32, (rows, PAIR), 0) < length
        grad_keys = jnp.where(masks[0], totals[0][0], totals[1][0])
        grad_values = jnp.where(masks[0], totals[0][1], totals[1][1])
        grad_keys = grad_keys * (1.0 / math.sqrt(HEAD_DIM))
        dk_ref[...] = jnp.where(usable, grad_keys, 0.0).astype(BF16)
        dv_ref[...] = jnp.where(usable, grad_values, 0.0).astype(BF16)


def kernel_call(body, place, operands, in_specs, outs, out_specs, pairs, scratch, flops):
    return pl.pallas_call(
        body,
        grid_spec=pltpu.PrefetchScalarGridSpec(
            num_scalar_prefetch=1,
            grid=(pairs,),
            in_specs=in_specs,
            out_specs=out_specs,
            scratch_shapes=scratch,
        ),
        out_shape=outs,
        compiler_params=pltpu.CompilerParams(vmem_limit_bytes=48 * 1024 * 1024),
        cost_estimate=pl.CostEstimate(flops=flops, bytes_accessed=10_000_000, transcendentals=0),
    )(place, *operands)


def mix_specs(number, tokens, pairs):
    def own(part):
        return pl.BlockSpec((1, tokens, PAIR), lambda h, place: (place[0], 0, part * pairs + h))

    def every(part):
        return pl.BlockSpec((number, tokens, PAIR), lambda h, place: (0, 0, part * pairs + h))

    return own, every


def attend_forward(place, mix):
    number, tokens, width = mix.shape
    model_width = width // 3
    pairs = model_width // PAIR
    own, every = mix_specs(number, tokens, pairs)
    chunk = CHUNK_BLOCKS * tokens
    block = pl.BlockSpec((tokens, PAIR), lambda h, place: (0, h))
    return kernel_call(
        forward_kernel,
        place,
        (mix, mix, mix),
        [own(0), every(1), every(2)],
        (
            jax.ShapeDtypeStruct((tokens, model_width), F32),
            jax.ShapeDtypeStruct((tokens, model_width), BF16),
            jax.ShapeDtypeStruct((tokens, model_width), F32),
            jax.ShapeDtypeStruct((pairs, 2, tokens), F32),
        ),
        (block, block, block, pl.BlockSpec((1, 2, tokens), lambda h, place: (h, 0, 0))),
        pairs,
        [pltpu.VMEM((2, number // CHUNK_BLOCKS, tokens, chunk), F32)],
        8 * number * tokens * tokens * model_width,
    )


def attend_queries(place, mix, grads, attended, column):
    number, tokens, width = mix.shape
    model_width = width // 3
    pairs = model_width // PAIR
    own, every = mix_specs(number, tokens, pairs)
    block = pl.BlockSpec((tokens, PAIR), lambda h, place: (0, h))
    return kernel_call(
        query_kernel,
        place,
        (mix, mix, mix, grads, attended, column),
        [own(0), every(1), every(2), block, block, block],
        jax.ShapeDtypeStruct((tokens, model_width), BF16),
        block,
        pairs,
        [],
        12 * number * tokens * tokens * model_width,
    )


def attend_keys(place, mix, all_grads, stats):
    number, tokens, width = mix.shape
    model_width = width // 3
    pairs = model_width // PAIR
    own, every = mix_specs(number, tokens, pairs)
    block = pl.BlockSpec((tokens, PAIR), lambda h, place: (0, h))
    return kernel_call(
        key_kernel,
        place,
        (mix, mix, mix, all_grads, stats),
        [
            own(1),
            own(2),
            every(0),
            every(0),
            pl.BlockSpec((number, 1, 4, tokens), lambda h, place: (0, h, 0, 0)),
        ],
        (
            jax.ShapeDtypeStruct((tokens, model_width), BF16),
            jax.ShapeDtypeStruct((tokens, model_width), BF16),
        ),
        (block, block),
        pairs,
        [],
        16 * number * tokens * tokens * model_width,
    )


def on_device(
    hidden_states,
    lengths,
    cotangent,
    attend_weight,
    query_bias,
    value_bias,
    output_weight,
    output_bias,
    first_gain,
    first_shift,
    raise_weight,
    raise_bias,
    lower_weight,
    lower_bias,
    second_gain,
    second_shift,
):
    seq_count, tok_count, model_width = hidden_states.shape
    row_count = seq_count * tok_count
    block_shape = (seq_count, tok_count, model_width)
    number = lax.axis_size("ctx")
    pairs = model_width // PAIR
    me = lax.axis_index("ctx")
    chips = ctx_bits()
    orders = (chips + [1], chips[::-1] + [1])

    def gather_tokens(blocked):
        return [gather_ctx(blocked[at], orders[at % 2]) for at in range(seq_count)]

    tokens_all = gather_tokens(hidden_states)
    attend_full = gather_weight_core(attend_weight)
    (
        query_add,
        value_add,
        output_add,
        gain_first,
        shift_first,
        raise_add,
        lower_add,
        gain_second,
        shift_second,
    ) = gather_vectors(
        [
            query_bias,
            value_bias,
            output_bias,
            first_gain,
            first_shift,
            raise_bias,
            lower_bias,
            second_gain,
            second_shift,
        ]
    )
    output_full = gather_weight_core(output_weight)
    raise_full = gather_weight_ctx(raise_weight)
    lower_full = gather_weight_ctx(lower_weight)

    mix_add = jnp.concatenate([query_add, jnp.zeros_like(query_add), value_add])
    places = [
        jnp.stack([me.astype(jnp.int32), lengths[at].astype(jnp.int32)]) for at in range(seq_count)
    ]
    mixes = []
    for at in range(seq_count):
        mixed = jnp.dot(
            tokens_all[at].reshape(number * tok_count, model_width),
            attend_full,
            preferred_element_type=F32,
        )
        mixes.append((mixed + mix_add).astype(BF16).reshape(number, tok_count, 3 * model_width))
    attended, attended_lows, columns, lse_rows = zip(
        *[attend_forward(places[at], mixes[at]) for at in range(seq_count)]
    )
    attended_low = jnp.concatenate(attended_lows, axis=0)

    token_rows = hidden_states.reshape(row_count, model_width)
    projected = jnp.dot(attended_low, output_full, preferred_element_type=F32) + output_add
    normed_first, first_back = jax.vjp(
        layer_norm, token_rows.astype(F32) + projected, gain_first, shift_first
    )
    first_low = normed_first.astype(BF16)
    raised = jnp.dot(first_low, raise_full, preferred_element_type=F32) + raise_add
    active, gelu_back = jax.vjp(gelu_exact, raised)
    active_low = active.astype(BF16)
    lowered = jnp.dot(active_low, lower_full, preferred_element_type=F32) + lower_add
    result, second_back = jax.vjp(layer_norm, normed_first + lowered, gain_second, shift_second)
    layer_output = result.astype(BF16).reshape(block_shape)
    grad_out = cotangent.reshape(row_count, model_width).astype(F32)
    grad_mid, grad_gain_second, grad_shift_second = second_back(grad_out)
    mid_low = grad_mid.astype(BF16)
    grad_lower_weight = jnp.einsum("rf,rd->fd", active_low, mid_low, preferred_element_type=F32)
    grad_lower_add = jnp.sum(mid_low.astype(F32), axis=0)
    grad_active = jnp.einsum("rd,fd->rf", mid_low, lower_full, preferred_element_type=F32)
    (grad_raised,) = gelu_back(grad_active)
    raised_low = grad_raised.astype(BF16)
    grad_raise_weight = jnp.einsum("rd,rf->df", first_low, raised_low, preferred_element_type=F32)
    grad_raise_add = jnp.sum(raised_low.astype(F32), axis=0)
    grad_first = grad_mid + jnp.einsum(
        "rf,df->rd", raised_low, raise_full, preferred_element_type=F32
    )
    grad_resid, grad_gain_first, grad_shift_first = first_back(grad_first)
    resid_low = grad_resid.astype(BF16)
    grad_output_weight = jnp.einsum(
        "rc,rd->cd", attended_low, resid_low, preferred_element_type=F32
    )
    grad_output_add = jnp.sum(resid_low.astype(F32), axis=0)
    grad_att = (
        jnp.einsum("rd,cd->rc", resid_low, output_full, preferred_element_type=F32)
        .astype(BF16)
        .reshape(block_shape)
    )
    grads_all = gather_tokens(grad_att)
    head_of = lax.broadcasted_iota(jnp.int32, (HEADS, model_width), 1) // HEAD_DIM
    pick = (head_of == lax.broadcasted_iota(jnp.int32, (HEADS, model_width), 0)).astype(F32)
    query_grads, key_grads, value_grads = [], [], []
    stats_all = []
    for at in range(seq_count):
        delta = jnp.einsum(
            "hd,td->ht",
            pick,
            grad_att[at].astype(F32) * attended[at],
            precision=lax.Precision.HIGHEST,
            preferred_element_type=F32,
        ).reshape(pairs, 2, tok_count)
        stats_all.append(
            gather_ctx(jnp.concatenate([lse_rows[at], delta], axis=1), orders[at % 2])
        )
    for at in range(seq_count):
        query_grads.append(
            attend_queries(places[at], mixes[at], grad_att[at], attended[at], columns[at])
        )
    for at in range(seq_count):
        grad_keys, grad_values = attend_keys(places[at], mixes[at], grads_all[at], stats_all[at])
        key_grads.append(grad_keys)
        value_grads.append(grad_values)
    query_low = jnp.concatenate(query_grads, axis=0)
    key_low = jnp.concatenate(key_grads, axis=0)
    value_low = jnp.concatenate(value_grads, axis=0)
    grad_mixture = jnp.concatenate([query_low, key_low, value_low], axis=1)
    grad_attend_weight = jnp.einsum(
        "rd,rc->dc", token_rows, grad_mixture, preferred_element_type=F32
    )
    grad_query_add = jnp.sum(query_low.astype(F32), axis=0)
    grad_value_add = jnp.sum(value_low.astype(F32), axis=0)
    hidden_grad = grad_resid + jnp.einsum(
        "rc,dc->rd", grad_mixture, attend_full, preferred_element_type=F32
    )
    (
        grad_output_add,
        grad_gain_first,
        grad_shift_first,
        grad_raise_add,
        grad_lower_add,
        grad_gain_second,
        grad_shift_second,
    ) = sum_vectors(
        [
            grad_output_add,
            grad_gain_first,
            grad_shift_first,
            grad_raise_add,
            grad_lower_add,
            grad_gain_second,
            grad_shift_second,
        ]
    )
    grad_query_add, grad_value_add = sum_vectors([grad_query_add, grad_value_add])
    return (
        layer_output,
        hidden_grad.reshape(block_shape),
        sum_weight(grad_attend_weight),
        grad_query_add,
        grad_value_add,
        sum_weight(grad_output_weight),
        grad_output_add,
        grad_gain_first,
        grad_shift_first,
        sum_weight(grad_raise_weight),
        grad_raise_add,
        sum_weight(grad_lower_weight),
        grad_lower_add,
        grad_gain_second,
        grad_shift_second,
    )


def solution(mesh):
    return jax.shard_map(
        on_device,
        mesh=mesh,
        in_specs=(
            P("fsdp", "ctx", None),
            P("fsdp"),
            P("fsdp", "ctx", None),
            P("fsdp", None),
            P("fsdp"),
            P("fsdp"),
            P("fsdp", None),
            P("fsdp"),
            P("fsdp"),
            P("fsdp"),
            P("fsdp", None),
            P("fsdp"),
            P("fsdp", None),
            P("fsdp"),
            P("fsdp"),
            P("fsdp"),
        ),
        out_specs=(
            P("fsdp", "ctx", None),
            P("fsdp", "ctx", None),
            P("fsdp", None),
            P("fsdp"),
            P("fsdp"),
            P("fsdp", None),
            P("fsdp"),
            P("fsdp"),
            P("fsdp"),
            P("fsdp", None),
            P("fsdp"),
            P("fsdp", None),
            P("fsdp"),
            P("fsdp"),
            P("fsdp"),
        ),
        check_vma=False,
    )
```

time: 1230 us -> 674 us (0.55)
  waiting for transfers between devices: 781 us -> 229 us
  matrix products: 221 us -> 78.9 us
  Pallas kernels: 0 us -> 136 us
  starting transfers between devices: 0.74 us -> 104 us
  blocking collectives: 93.3 us -> 0 us
  between operations: 17.2 us -> 3.62 us
    reduce_scatter x3 -> x0, waiting for transfers between devices: 375 us -> none  [the longest x1 164 us: on_device(): lax.psum_scatter(summed_all[9], 'fsdp', scatter_dimension=0, tiled=True)]
    ppermute x0 -> x143, waiting for transfers between devices: none -> 229 us  [the longest x110 145 us: swap(): return lax.ppermute(value, 'ctx', [(at, at ^ bit) for at in range(number)])]
    all_gather x8 -> x0, waiting for transfers between devices: 229 us -> none  [the longest x1 79.1 us: on_device(): lax.all_gather(raise_weight, 'fsdp', axis=0, tiled=True)]
    dot_general x16 -> x13, matrix products: 210 us -> 71.4 us  [the longest x2 19.5 us: on_device(): jnp.dot(tokens_all[at].reshape(number * tok_count, model_width), attend_f...]
    pallas_call x0 -> x6, Pallas kernels: none -> 136 us  [kernel_call(): pl.pallas_call(body, grid_spec=pltpu.PrefetchScalarGridSpec(num_scalar_pr...]
    ppermute x0 -> x143, starting transfers between devices: none -> 104 us  [the longest x110 75.7 us: swap(): return lax.ppermute(value, 'ctx', [(at, at ^ bit) for at in range(number)])]
    unnamed x14 -> x0, waiting for transfers between devices: 103 us -> none
    psum x1 -> x0, waiting for transfers between devices: 74 us -> none  [on_device(): lax.psum((grad_attend_weight, grad_query_add, grad_value_add, grad_output...]
  transfers between devices with their start and end apart: 13 -> 143, of which waited for: 9 -> 76; matrix products, arithmetic and copies ran while one was open for 19% -> 16% of each run, Pallas kernels for 0% -> 17%
where the time goes in v1:
time: 674 us; the launch traced here: 665 us
  waiting for transfers between devices  229 us (34%)
  Pallas kernels  136 us (20%)
  starting transfers between devices  104 us (15%)
  matrix products  78.9 us (12%)
  local copies, waits for them, and re-layouts  70.6 us (10%)
  other arithmetic  43.2 us (6%)
    ppermute x110, waiting for transfers between devices, swap(): return lax.ppermute(value, 'ctx', [(at, at ^ bit) for at in range(number)])  145 us
    pallas_call x6, Pallas kernels, kernel_call(): pl.pallas_call(body, grid_spec=pltpu.PrefetchScalarGridSpec(num_scalar_pr...  136 us
    ppermute x33, waiting for transfers between devices, shift_fsdp(): lax.ppermute(value, 'fsdp', [(at, (at + step) % number) for at in range(n...  84.4 us
    ppermute x110, starting transfers between devices, swap(): return lax.ppermute(value, 'ctx', [(at, at ^ bit) for at in range(number)])  75.7 us
    ppermute x33, starting transfers between devices, shift_fsdp(): lax.ppermute(value, 'fsdp', [(at, (at + step) % number) for at in range(n...  28.2 us
    dot_general x2, matrix products, on_device(): jnp.dot(tokens_all[at].reshape(number * tok_count, model_width), attend_f...  19.5 us
    dot_general x1, matrix products, on_device(): jnp.dot(first_low, raise_full, preferred_element_type=F32) + raise_add  18.3 us
    another operation x137, other arithmetic, gather_ctx(): jnp.stack([jnp.where(high, other, held), jnp.where(high, held, other)], a...  17.6 us
  transfers between devices with their start and end apart: 143, of which 76 were waited for; matrix products, arithmetic and copies ran while one was open for 16% of the time, Pallas kernels for 17%

profile of v1, /device:TPU:0, one launch (start us, length us, event | category | flops | bytes accessed | tf_op | source)
XLA Modules:
  0.0 665.2 jit_solution(9730939698750686137)
XLA Ops:
  0.7 6.3 concatenate.77
  43.4 12.0 %collective-permute-done.21 = bf16[24,3072]{1,0:T(8,128)(2,1)S(1)} collective-permute-done((bf16[24,3072]{1,0:T(8,128)(2,1)S(1)}, bf16[24,3072]{1,0:T(8,128)(2,1)S(1)}, u32[]{:S(2)}, u32[]{:S(2)}) %collective-permute-start.21) | collective-permute-done | bytes 147488 | tf_op jit(solution)/shard_map/ppermute | solution.py:40
  56.6 5.7 collective-permute-done.42
  71.1 6.8 %collective-permute-done.28 = bf16[24,3072]{1,0:T(8,128)(2,1)S(1)} collective-permute-done((bf16[24,3072]{1,0:T(8,128)(2,1)S(1)}, bf16[24,3072]{1,0:T(8,128)(2,1)S(1)}, u32[]{:S(2)}, u32[]{:S(2)}) %collective-permute-start.28) | collective-permute-done | bytes 147488 | tf_op jit(solution)/shard_map/ppermute | solution.py:40
  78.7 6.2 collective-permute-done.17
  87.0 4.6 collective-permute-done.26
  110.7 7.3 %collective-permute-done.35 = bf16[24,3072]{1,0:T(8,128)(2,1)S(1)} collective-permute-done((bf16[24,3072]{1,0:T(8,128)(2,1)S(1)}, bf16[24,3072]{1,0:T(8,128)(2,1)S(1)}, u32[]{:S(2)}, u32[]{:S(2)}) %collective-permute-start.35) | collective-permute-done | bytes 147488 | tf_op jit(solution)/shard_map/ppermute | solution.py:40
  134.7 4.9 collective-permute-done.37
  151.6 17.2 %collective-permute-done.58 = bf16[2,96,384]{2,1,0:T(8,128)(2,1)S(1)} collective-permute-done((bf16[2,96,384]{2,1,0:T(8,128)(2,1)S(1)}, bf16[2,96,384]{2,1,0:T(8,128)(2,1)S(1)}, u32[]{:S(2)}, u32[]{:S(2)}) %collective-permute-start.58) | collective-permute-done | bytes 147488 | tf_op jit(solution)/shard_map/ppermute | solution.py:35
  175.7 6.3 collective-permute-done.5
  195.8 5.5 collective-permute-done.7
  203.9 9.8 %add_convert_fusion.1 = bf16[2048,2304]{1,0:T(8,128)(2,1)} fusion(bf16[2048,768]{1,0:T(8,128)(2,1)S(1)} %bitcast.652, bf16[768,2304]{1,0:T(8,128)(2,1)S(1)} %bitcast.648, f32[2304]{0:T(1024)S(1)} %pad_maximum_fusion.81), kind=kOutput, calls=%fused_computation.1 | convolution fusion | flops 7257194496 | bytes 16131072 | tf_op jit(solution)/shard_map/dot_general | solution.py:495
  213.6 21.4 %shard_map.271 = (f32[256,768]{1,0:T(8,128)S(1)}, bf16[256,768]{1,0:T(8,128)(2,1)S(1)}, f32[256,768]{1,0:T(8,128)S(1)}, f32[6,2,256]{2,1,0:T(2,128)S(1)}) custom-call(s32[2]{0:T(128)S(1)} %get-tuple-element.317.place_ref, bf16[8,256,2304]{2,1,0:T(8,128)(2,1)} %bitcast.616, bf16[8,256,2304]{2,1,0:T(8,128)(2,1)} %bitcast.617, bf16[8,256,2304]{2,1,0:T(8,128)(2,1)} %bitcast.618), custom_call_target="tpu_custom_call" | custom-call | flops 3221225472 | bytes 10000000 | tf_op jit(solution)/shard_map/pallas_call | solution.py:333
  237.7 9.7 %add_convert_fusion = bf16[2048,2304]{1,0:T(8,128)(2,1)} fusion(bf16[2048,768]{1,0:T(8,128)(2,1)S(1)} %bitcast.651, bf16[768,2304]{1,0:T(8,128)(2,1)S(1)} %bitcast.649, f32[2304]{0:T(1024)S(1)} %copy-done.60), kind=kOutput, calls=%fused_computation | convolution fusion | flops 7257194496 | bytes 16131072 | tf_op jit(solution)/shard_map/dot_general | solution.py:495
  247.4 21.8 %shard_map.272 = (f32[256,768]{1,0:T(8,128)S(1)}, bf16[256,768]{1,0:T(8,128)(2,1)S(1)}, f32[256,768]{1,0:T(8,128)S(1)}, f32[6,2,256]{2,1,0:T(2,128)S(1)}) custom-call(s32[2]{0:T(128)S(1)} %get-tuple-element.318.place_ref, bf16[8,256,2304]{2,1,0:T(8,128)(2,1)} %bitcast.625, bf16[8,256,2304]{2,1,0:T(8,128)(2,1)} %bitcast.626, bf16[8,256,2304]{2,1,0:T(8,128)(2,1)} %bitcast.627), custom_call_target="tpu_custom_call" | custom-call | flops 3221225472 | bytes 10000000 | tf_op jit(solution)/shard_map/pallas_call | solution.py:333
  270.7 18.3 %multiply_convert_fusion = (bf16[512,3072]{1,0:T(8,128)(2,1)S(1)}, f32[512,3072]{1,0:T(8,128)S(1)}, f32[512,3072]{1,0:T(8,128)S(1)}) fusion(f32[3072]{0:T(1024)S(1)} %copy-done.45, bf16[768,3072]{1,0:T(8,128)(2,1)} %bitcast.644, f32[512,768]{1,0:T(8,128)S(1)} %get-tuple-element.314, f32[768]{0:T(1024)S(1)} %copy-done.63, f32[768]{0:T(1024)S(1)} %copy-done.58, ...), kind=kOutput, calls=%fused_computation.6 | convolution fusion | flops 2521694208 | bytes 22042624 | tf_op jit(solution)/shard_map/dot_general | solution.py:512
  289.0 6.2 fusion.113
  299.3 4.8 fusion.134
  307.8 6.1 multiply_reduce_fusion
  319.5 5.5 fusion.107
  325.0 5.1 fusion.136
  338.9 21.4 %shard_map.274 = bf16[256,768]{1,0:T(8,128)(2,1)S(1)} custom-call(s32[2]{0:T(128)S(1)} %get-tuple-element.318.place_ref, bf16[8,256,2304]{2,1,0:T(8,128)(2,1)} %bitcast.628, bf16[8,256,2304]{2,1,0:T(8,128)(2,1)} %bitcast.629, bf16[8,256,2304]{2,1,0:T(8,128)(2,1)} %bitcast.630, bf16[256,768]{1,0:T(8,128)(2,1)S(1)} %get-tuple-element.101.g_ref, ...), custom_call_target="tpu_custom_call" | custom-call | flops 4831838208 | bytes 10000000 | tf_op jit(solution)/shard_map/pallas_call | solution.py:333
  360.3 21.4 %shard_map.273 = bf16[256,768]{1,0:T(8,128)(2,1)S(1)} custom-call(s32[2]{0:T(128)S(1)} %copy-done.5, bf16[8,256,2304]{2,1,0:T(8,128)(2,1)} %bitcast.619, bf16[8,256,2304]{2,1,0:T(8,128)(2,1)} %bitcast.620, bf16[8,256,2304]{2,1,0:T(8,128)(2,1)} %bitcast.621, bf16[256,768]{1,0:T(8,128)(2,1)S(1)} %get-tuple-element.102.g_ref, ...), custom_call_target="tpu_custom_call" | custom-call | flops 4831838208 | bytes 10000000 | tf_op jit(solution)/shard_map/pallas_call | solution.py:333
  439.6 10.6 %collective-permute-done.103 = bf16[24,384]{1,0:T(8,128)(2,1)S(1)} collective-permute-done((bf16[24,384]{1,0:T(8,128)(2,1)S(1)}, bf16[24,384]{1,0:T(8,128)(2,1)S(1)}, u32[]{:S(2)}, u32[]{:S(2)}) %collective-permute-start.103) | collective-permute-done | bytes 18464 | tf_op jit(solution)/shard_map/ppermute | solution.py:35
  456.3 9.7 %collective-permute-done.104 = bf16[2,24,384]{2,1,0:T(8,128)(2,1)S(1)} collective-permute-done((bf16[2,24,384]{2,1,0:T(8,128)(2,1)S(1)}, bf16[2,24,384]{2,1,0:T(8,128)(2,1)S(1)}, u32[]{:S(2)}, u32[]{:S(2)}) %collective-permute-start.104) | collective-permute-done | bytes 36896 | tf_op jit(solution)/shard_map/ppermute | solution.py:35
  482.4 24.8 %shard_map.275 = (bf16[256,768]{1,0:T(8,128)(2,1)S(1)}, bf16[256,768]{1,0:T(8,128)(2,1)S(1)}) custom-call(s32[2]{0:T(128)S(1)} %copy-done.6, bf16[8,256,2304]{2,1,0:T(8,128)(2,1)} %bitcast.622, bf16[8,256,2304]{2,1,0:T(8,128)(2,1)} %bitcast.623, bf16[8,256,2304]{2,1,0:T(8,128)(2,1)} %bitcast.624, bf16[8,256,768]{2,1,0:T(8,128)(2,1)S(1)} %bitcast.612, ...), custom_call_target="tpu_custom_call" | custom-call | flops 6442450944 | bytes 10000000 | tf_op jit(solution)/shard_map/pallas_call | solution.py:333
  509.4 24.8 %shard_map.276 = (bf16[256,768]{1,0:T(8,128)(2,1)S(1)}, bf16[256,768]{1,0:T(8,128)(2,1)S(1)}) custom-call(s32[2]{0:T(128)S(1)} %get-tuple-element.318.place_ref, bf16[8,256,2304]{2,1,0:T(8,128)(2,1)} %bitcast.631, bf16[8,256,2304]{2,1,0:T(8,128)(2,1)} %bitcast.632, bf16[8,256,2304]{2,1,0:T(8,128)(2,1)} %bitcast.633, bf16[8,256,768]{2,1,0:T(8,128)(2,1)S(1)} %bitcast.613, ...), custom_call_target="tpu_custom_call" | custom-call | flops 6442450944 | bytes 10000000 | tf_op jit(solution)/shard_map/pallas_call | solution.py:333
  537.7 5.5 add_add_fusion.4
  561.7 6.4 collective-permute-done.130
  572.6 5.0 collective-permute-done.117
  586.6 10.2 %collective-permute-done.121 = bf16[24,3072]{1,0:T(8,128)(2,1)S(1)} collective-permute-done((bf16[24,3072]{1,0:T(8,128)(2,1)S(1)}, bf16[24,3072]{1,0:T(8,128)(2,1)S(1)}, u32[]{:S(2)}, u32[]{:S(2)}) %collective-permute-start.121) | collective-permute-done | bytes 147488 | tf_op jit(solution)/shard_map/ppermute | solution.py:40
  621.5 10.1 %collective-permute-done.76 = bf16[4,2,24,1152]{3,2,0,1:T(8,128)(2,1)S(1)} collective-permute-done((bf16[4,2,24,1152]{3,2,0,1:T(8,128)(2,1)S(1)}, bf16[4,2,24,1152]{3,2,0,1:T(8,128)(2,1)S(1)}, u32[]{:S(2)}, u32[]{:S(2)}) %collective-permute-start.76) | collective-permute-done | bytes 442400 | tf_op jit(solution)/shard_map/ppermute | solution.py:35
  (775 shorter events, 320.1 us)
Async XLA Ops:
  6.9 29.6 %collective-permute-start.9 = (bf16[1,2304]{1,0:T(2,128)(2,1)S(1)}, bf16[1,2304]{1,0:T(2,128)(2,1)S(1)}, u32[]{:S(2)}, u32[]{:S(2)}) collective-permute-start(bf16[1,2304]{1,0:T(2,128)(2,1)S(1)} %broadcast_in_dim.90), channel_id=1, source_target_pairs={{0,1},{1,2},{2,3},{3,0},{4,5},{5,6},{6,7},{7,4},{8,9},{9,10},{10,1... | collective-permute-start | bytes 13832 | tf_op jit(solution)/shard_map/ppermute | solution.py:40
  10.0 27.3 %collective-permute-start.10 = (bf16[1,2304]{1,0:T(2,128)(2,1)S(1)}, bf16[1,2304]{1,0:T(2,128)(2,1)S(1)}, u32[]{:S(2)}, u32[]{:S(2)}) collective-permute-start(bf16[1,2304]{1,0:T(2,128)(2,1)S(1)} %broadcast_in_dim.90), channel_id=1, source_target_pairs={{0,2},{1,3},{2,0},{3,1},{4,6},{5,7},{6,4},{7,5},{8,10},{9,11},{10,... | collective-permute-start | bytes 13832 | tf_op jit(solution)/shard_map/ppermute | solution.py:40
  12.6 25.0 %collective-permute-start.11 = (bf16[1,2304]{1,0:T(2,128)(2,1)S(1)}, bf16[1,2304]{1,0:T(2,128)(2,1)S(1)}, u32[]{:S(2)}, u32[]{:S(2)}) collective-permute-start(bf16[1,2304]{1,0:T(2,128)(2,1)S(1)} %broadcast_in_dim.90), channel_id=1, source_target_pairs={{0,3},{1,0},{2,1},{3,2},{4,7},{5,4},{6,5},{7,6},{8,11},{9,8},{10,9... | collective-permute-start | bytes 13832 | tf_op jit(solution)/shard_map/ppermute | solution.py:40
  16.0 90.5 %collective-permute-start.12 = (bf16[256,768]{1,0:T(8,128)(2,1)}, bf16[256,768]{1,0:T(8,128)(2,1)}, u32[]{:S(2)}, u32[]{:S(2)}) collective-permute-start(bf16[256,768]{1,0:T(8,128)(2,1)} %get-tuple-element.105), channel_id=1, source_target_pairs={{0,16},{4,20},{8,24},{12,28},{16,0},{20,4},{24,8},{28,12},{1,17},{... | collective-permute-start | bytes 1179656 | tf_op jit(solution)/shard_map/ppermute | solution.py:35
  17.5 89.0 %collective-permute-start = (bf16[256,768]{1,0:T(8,128)(2,1)}, bf16[256,768]{1,0:T(8,128)(2,1)}, u32[]{:S(2)}, u32[]{:S(2)}) collective-permute-start(bf16[256,768]{1,0:T(8,128)(2,1)} %get-tuple-element.106), channel_id=1, source_target_pairs={{0,8},{4,12},{8,0},{12,4},{16,24},{20,28},{24,16},{28,20},{1,9},{5... | collective-permute-start | bytes 1179656 | tf_op jit(solution)/shard_map/ppermute | solution.py:35
  36.5 72.5 %collective-permute-start.3 = (bf16[96,2304]{1,0:T(8,128)(2,1)}, bf16[96,2304]{1,0:T(8,128)(2,1)}, u32[]{:S(2)}, u32[]{:S(2)}) collective-permute-start(bf16[96,2304]{1,0:T(8,128)(2,1)} %dynamic-slice_bitcast_fusion.5), channel_id=1, source_target_pairs={{0,1},{1,2},{2,3},{3,0},{4,5},{5,6},{6,7},{7,4},{8,9},{9,10},{10,1... | collective-permute-start | bytes 1327112 | tf_op jit(solution)/shard_map/ppermute | solution.py:40
  37.3 18.1 %collective-permute-start.15 = (bf16[96,768]{1,0:T(8,128)(2,1)}, bf16[96,768]{1,0:T(8,128)(2,1)S(1)}, u32[]{:S(2)}, u32[]{:S(2)}) collective-permute-start(bf16[96,768]{1,0:T(8,128)(2,1)} %dynamic-slice_bitcast_fusion.15), channel_id=1, source_target_pairs={{0,1},{1,2},{2,3},{3,0},{4,5},{5,6},{6,7},{7,4},{8,9},{9,10},{10,1... | collective-permute-start | bytes 442376 | tf_op jit(solution)/shard_map/ppermute | solution.py:40
  37.7 17.7 %collective-permute-start.21 = (bf16[24,3072]{1,0:T(8,128)(2,1)S(1)}, bf16[24,3072]{1,0:T(8,128)(2,1)S(1)}, u32[]{:S(2)}, u32[]{:S(2)}) collective-permute-start(bf16[24,3072]{1,0:T(8,128)(2,1)S(1)} %copy-done.40), channel_id=1, source_target_pairs={{0,1},{1,2},{2,3},{3,0},{4,5},{5,6},{6,7},{7,4},{8,9},{9,10},{10,1... | collective-permute-start | bytes 442376 | tf_op jit(solution)/shard_map/ppermute | solution.py:40
  109.0 24.5 %collective-permute-start.24 = (bf16[2,2,24,1536]{3,2,1,0:T(8,128)(2,1)S(1)}, bf16[2,2,24,1536]{3,2,1,0:T(8,128)(2,1)S(1)}, u32[]{:S(2)}, u32[]{:S(2)}) collective-permute-start(bf16[2,2,24,1536]{3,2,1,0:T(8,128)(2,1)S(1)} %pad_maximum_fusion.31), channel_id=1, source_target_pairs={{0,4},{4,0},{8,12},{12,8},{16,20},{20,16},{24,28},{28,24},{1,5},{5... | collective-permute-start | bytes 884744 | tf_op jit(solution)/shard_map/ppermute | solution.py:35
  118.0 28.1 %collective-permute-start.27 = (bf16[2,2,24,1536]{3,2,0,1:T(8,128)(2,1)S(1)}, bf16[2,2,24,1536]{3,2,0,1:T(8,128)(2,1)S(1)}, u32[]{:S(2)}, u32[]{:S(2)}) collective-permute-start(bf16[2,2,24,1536]{3,2,0,1:T(8,128)(2,1)S(1)} %pad_maximum_fusion.32), channel_id=1, source_target_pairs={{0,4},{4,0},{8,12},{12,8},{16,20},{20,16},{24,28},{28,24},{1,5},{5... | collective-permute-start | bytes 884744 | tf_op jit(solution)/shard_map/ppermute | solution.py:35
  118.0 16.5 %collective-permute-start.30 = (bf16[2,24,1536]{2,1,0:T(8,128)(2,1)S(1)}, bf16[2,24,1536]{2,1,0:T(8,128)(2,1)S(1)}, u32[]{:S(2)}, u32[]{:S(2)}) collective-permute-start(bf16[2,24,1536]{2,1,0:T(8,128)(2,1)S(1)} %pad_maximum_fusion.53), channel_id=1, source_target_pairs={{0,16},{4,20},{8,24},{12,28},{16,0},{20,4},{24,8},{28,12},{1,17},{... | collective-permute-start | bytes 442376 | tf_op jit(solution)/shard_map/ppermute | solution.py:35
  144.9 26.2 %collective-permute-start.54 = (bf16[2,96,384]{2,1,0:T(8,128)(2,1)S(1)}, bf16[2,96,384]{2,1,0:T(8,128)(2,1)S(1)}, u32[]{:S(2)}, u32[]{:S(2)}) collective-permute-start(bf16[2,96,384]{2,1,0:T(8,128)(2,1)S(1)} %pad_maximum_fusion.60), channel_id=1, source_target_pairs={{0,8},{4,12},{8,0},{12,4},{16,24},{20,28},{24,16},{28,20},{1,9},{5... | collective-permute-start | bytes 442376 | tf_op jit(solution)/shard_map/ppermute | solution.py:35
  146.1 48.5 %collective-permute-start.13 = (bf16[2,256,768]{2,1,0:T(8,128)(2,1)S(1)}, bf16[2,256,768]{2,1,0:T(8,128)(2,1)S(1)}, u32[]{:S(2)}, u32[]{:S(2)}) collective-permute-start(bf16[2,256,768]{2,1,0:T(8,128)(2,1)S(1)} %pad_maximum_fusion.10), channel_id=1, source_target_pairs={{0,8},{4,12},{8,0},{12,4},{16,24},{20,28},{24,16},{28,20},{1,9},{5... | collective-permute-start | bytes 2359304 | tf_op jit(solution)/shard_map/ppermute | solution.py:35
  148.1 46.5 %collective-permute-start.1 = (bf16[2,256,768]{2,1,0:T(8,128)(2,1)S(1)}, bf16[2,256,768]{2,1,0:T(8,128)(2,1)S(1)}, u32[]{:S(2)}, u32[]{:S(2)}) collective-permute-start(bf16[2,256,768]{2,1,0:T(8,128)(2,1)S(1)} %pad_maximum_fusion.9), channel_id=1, source_target_pairs={{0,16},{4,20},{8,24},{12,28},{16,0},{20,4},{24,8},{28,12},{1,17},{... | collective-permute-start | bytes 2359304 | tf_op jit(solution)/shard_map/ppermute | solution.py:35
  149.4 19.4 %collective-permute-start.58 = (bf16[2,96,384]{2,1,0:T(8,128)(2,1)S(1)}, bf16[2,96,384]{2,1,0:T(8,128)(2,1)S(1)}, u32[]{:S(2)}, u32[]{:S(2)}) collective-permute-start(bf16[2,96,384]{2,1,0:T(8,128)(2,1)S(1)} %pad_maximum_fusion.61), channel_id=1, source_target_pairs={{0,16},{4,20},{8,24},{12,28},{16,0},{20,4},{24,8},{28,12},{1,17},{... | collective-permute-start | bytes 442376 | tf_op jit(solution)/shard_map/ppermute | solution.py:35
  151.5 23.6 %collective-permute-start.4 = (bf16[96,2304]{1,0:T(8,128)(2,1)}, bf16[96,2304]{1,0:T(8,128)(2,1)S(1)}, u32[]{:S(2)}, u32[]{:S(2)}) collective-permute-start(bf16[96,2304]{1,0:T(8,128)(2,1)} %collective-permute-done.3), channel_id=1, source_target_pairs={{0,4},{4,0},{8,12},{12,8},{16,20},{20,16},{24,28},{28,24},{1,5},{5... | collective-permute-start | bytes 1327112 | tf_op jit(solution)/shard_map/ppermute | solution.py:35
  195.3 39.8 %collective-permute-start.14 = (bf16[2,2,256,768]{3,2,0,1:T(8,128)(2,1)S(1)}, bf16[2,2,256,768]{3,2,0,1:T(8,128)(2,1)}, u32[]{:S(2)}, u32[]{:S(2)}) collective-permute-start(bf16[2,2,256,768]{3,2,0,1:T(8,128)(2,1)S(1)} %pad_maximum_fusion.6), channel_id=1, source_target_pairs={{0,4},{4,0},{8,12},{12,8},{16,20},{20,16},{24,28},{28,24},{1,5},{5... | collective-permute-start | bytes 4718600 | tf_op jit(solution)/shard_map/ppermute | solution.py:35
  330.2 86.7 %collective-permute-start.69 = (bf16[256,768]{1,0:T(8,128)(2,1)S(1)}, bf16[256,768]{1,0:T(8,128)(2,1)}, u32[]{:S(2)}, u32[]{:S(2)}) collective-permute-start(bf16[256,768]{1,0:T(8,128)(2,1)S(1)} %get-tuple-element.101.g_ref), channel_id=1, source_target_pairs={{0,16},{4,20},{8,24},{12,28},{16,0},{20,4},{24,8},{28,12},{1,17},{... | collective-permute-start | bytes 1179656 | tf_op jit(solution)/shard_map/ppermute | solution.py:35
  331.6 85.3 %collective-permute-start.63 = (bf16[256,768]{1,0:T(8,128)(2,1)S(1)}, bf16[256,768]{1,0:T(8,128)(2,1)}, u32[]{:S(2)}, u32[]{:S(2)}) collective-permute-start(bf16[256,768]{1,0:T(8,128)(2,1)S(1)} %get-tuple-element.102.g_ref), channel_id=1, source_target_pairs={{0,8},{4,12},{8,0},{12,4},{16,24},{20,28},{24,16},{28,20},{1,9},{5... | collective-permute-start | bytes 1179656 | tf_op jit(solution)/shard_map/ppermute | solution.py:35
  333.6 59.2 %collective-permute-start.66 = (f32[6,4,256]{2,1,0:T(4,128)}, f32[6,4,256]{2,1,0:T(4,128)}, u32[]{:S(2)}, u32[]{:S(2)}) collective-permute-start(f32[6,4,256]{2,1,0:T(4,128)} %pad_maximum_fusion.79), channel_id=1, source_target_pairs={{0,8},{4,12},{8,0},{12,4},{16,24},{20,28},{24,16},{28,20},{1,9},{5... | collective-permute-start | bytes 73736 | tf_op jit(solution)/shard_map/ppermute | solution.py:35
  337.0 58.0 %collective-permute-start.72 = (f32[6,4,256]{2,1,0:T(4,128)}, f32[6,4,256]{2,1,0:T(4,128)}, u32[]{:S(2)}, u32[]{:S(2)}) collective-permute-start(f32[6,4,256]{2,1,0:T(4,128)} %pad_maximum_fusion.80), channel_id=1, source_target_pairs={{0,16},{4,20},{8,24},{12,28},{16,0},{20,4},{24,8},{28,12},{1,17},{... | collective-permute-start | bytes 73736 | tf_op jit(solution)/shard_map/ppermute | solution.py:35
  409.4 62.5 %collective-permute-start.115 = (bf16[4,2,2,24,3072]{4,3,0,2,1:T(8,128)(2,1)}, bf16[4,2,2,24,3072]{4,3,0,2,1:T(8,128)(2,1)S(1)}, u32[]{:S(2)}, u32[]{:S(2)}) collective-permute-start(bf16[4,2,2,24,3072]{4,3,0,2,1:T(8,128)(2,1)} %fusion.9), channel_id=1, source_target_pairs={{0,4},{4,0},{8,12},{12,8},{16,20},{20,16},{24,28},{28,24},{1,5},{5... | collective-permute-start | bytes 7077896 | tf_op jit(solution)/shard_map/ppermute | solution.py:35
  415.4 61.1 %collective-permute-start.129 = (bf16[4,2,2,96,768]{4,3,0,2,1:T(8,128)(2,1)}, bf16[4,2,2,96,768]{4,3,0,2,1:T(8,128)(2,1)S(1)}, u32[]{:S(2)}, u32[]{:S(2)}) collective-permute-start(bf16[4,2,2,96,768]{4,3,0,2,1:T(8,128)(2,1)} %fusion.10), channel_id=1, source_target_pairs={{0,4},{4,0},{8,12},{12,8},{16,20},{20,16},{24,28},{28,24},{1,5},{5... | collective-permute-start | bytes 7077896 | tf_op jit(solution)/shard_map/ppermute | solution.py:35
  433.0 36.6 %collective-permute-start.64 = (bf16[2,256,768]{2,1,0:T(8,128)(2,1)S(1)}, bf16[2,256,768]{2,1,0:T(8,128)(2,1)S(1)}, u32[]{:S(2)}, u32[]{:S(2)}) collective-permute-start(bf16[2,256,768]{2,1,0:T(8,128)(2,1)S(1)} %pad_maximum_fusion.11), channel_id=1, source_target_pairs={{0,16},{4,20},{8,24},{12,28},{16,0},{20,4},{24,8},{28,12},{1,17},{... | collective-permute-start | bytes 2359304 | tf_op jit(solution)/shard_map/ppermute | solution.py:35
  450.2 19.9 %collective-permute-start.70 = (bf16[2,256,768]{2,1,0:T(8,128)(2,1)S(1)}, bf16[2,256,768]{2,1,0:T(8,128)(2,1)S(1)}, u32[]{:S(2)}, u32[]{:S(2)}) collective-permute-start(bf16[2,256,768]{2,1,0:T(8,128)(2,1)S(1)} %pad_maximum_fusion.12), channel_id=1, source_target_pairs={{0,8},{4,12},{8,0},{12,4},{16,24},{20,28},{24,16},{28,20},{1,9},{5... | collective-permute-start | bytes 2359304 | tf_op jit(solution)/shard_map/ppermute | solution.py:35
  471.5 35.8 %collective-permute-start.71 = (bf16[2,2,256,768]{3,2,0,1:T(8,128)(2,1)}, bf16[2,2,256,768]{3,2,0,1:T(8,128)(2,1)}, u32[]{:S(2)}, u32[]{:S(2)}) collective-permute-start(bf16[2,2,256,768]{3,2,0,1:T(8,128)(2,1)} %pad_maximum_fusion.8), channel_id=1, source_target_pairs={{0,4},{4,0},{8,12},{12,8},{16,20},{20,16},{24,28},{28,24},{1,5},{5... | collective-permute-start | bytes 4718600 | tf_op jit(solution)/shard_map/ppermute | solution.py:35
  473.9 83.2 %collective-permute-start.116 = (bf16[4,2,24,1536]{3,2,0,1:T(8,128)(2,1)}, bf16[4,2,24,1536]{3,2,0,1:T(8,128)(2,1)}, u32[]{:S(2)}, u32[]{:S(2)}) collective-permute-start(bf16[4,2,24,1536]{3,2,0,1:T(8,128)(2,1)} %dynamic-slice_bitcast_fusion.3), channel_id=1, source_target_pairs={{0,8},{4,12},{8,0},{12,4},{16,24},{20,28},{24,16},{28,20},{1,9},{5... | collective-permute-start | bytes 1769480 | tf_op jit(solution)/shard_map/ppermute | solution.py:35
  475.6 84.0 %collective-permute-start.118 = (bf16[4,2,24,1536]{3,2,0,1:T(8,128)(2,1)}, bf16[4,2,24,1536]{3,2,0,1:T(8,128)(2,1)}, u32[]{:S(2)}, u32[]{:S(2)}) collective-permute-start(bf16[4,2,24,1536]{3,2,0,1:T(8,128)(2,1)} %dynamic-slice_bitcast_fusion.2), channel_id=1, source_target_pairs={{0,16},{4,20},{8,24},{12,28},{16,0},{20,4},{24,8},{28,12},{1,17},{... | collective-permute-start | bytes 1769480 | tf_op jit(solution)/shard_map/ppermute | solution.py:35
  556.4 62.0 %collective-permute-start.75 = (bf16[4,2,2,24,2304]{4,3,2,1,0:T(8,128)(2,1)S(1)}, bf16[4,2,2,24,2304]{4,3,2,1,0:T(8,128)(2,1)S(1)}, u32[]{:S(2)}, u32[]{:S(2)}) collective-permute-start(bf16[4,2,2,24,2304]{4,3,2,1,0:T(8,128)(2,1)S(1)} %fusion.11), channel_id=1, source_target_pairs={{0,4},{4,0},{8,12},{12,8},{16,20},{20,16},{24,28},{28,24},{1,5},{5... | collective-permute-start | bytes 5308424 | tf_op jit(solution)/shard_map/ppermute | solution.py:35
  558.5 19.2 %collective-permute-start.117 = (bf16[4,24,1536]{2,1,0:T(8,128)(2,1)S(1)}, bf16[4,24,1536]{2,1,0:T(8,128)(2,1)S(1)}, u32[]{:S(2)}, u32[]{:S(2)}) collective-permute-start(bf16[4,24,1536]{2,1,0:T(8,128)(2,1)S(1)} %dynamic-slice_bitcast_fusion.9), channel_id=1, source_target_pairs={{0,16},{4,20},{8,24},{12,28},{16,0},{20,4},{24,8},{28,12},{1,17},{... | collective-permute-start | bytes 884744 | tf_op jit(solution)/shard_map/ppermute | solution.py:35
  560.9 16.9 %collective-permute-start.119 = (bf16[4,24,1536]{2,1,0:T(8,128)(2,1)S(1)}, bf16[4,24,1536]{2,1,0:T(8,128)(2,1)S(1)}, u32[]{:S(2)}, u32[]{:S(2)}) collective-permute-start(bf16[4,24,1536]{2,1,0:T(8,128)(2,1)S(1)} %dynamic-slice_bitcast_fusion.8), channel_id=1, source_target_pairs={{0,8},{4,12},{8,0},{12,4},{16,24},{20,28},{24,16},{28,20},{1,9},{5... | collective-permute-start | bytes 884744 | tf_op jit(solution)/shard_map/ppermute | solution.py:35
  579.8 16.9 %collective-permute-start.121 = (bf16[24,3072]{1,0:T(8,128)(2,1)S(1)}, bf16[24,3072]{1,0:T(8,128)(2,1)S(1)}, u32[]{:S(2)}, u32[]{:S(2)}) collective-permute-start(bf16[24,3072]{1,0:T(8,128)(2,1)S(1)} %get-tuple-element.119), channel_id=1, source_target_pairs={{0,2},{1,3},{2,0},{3,1},{4,6},{5,7},{6,4},{7,5},{8,10},{9,11},{10,... | collective-permute-start | bytes 442376 | tf_op jit(solution)/shard_map/ppermute | solution.py:40
  (189 other events, 1810.5 us)

commit v2 on v1

--- a/solution.py
+++ b/solution.py
@@ -17,6 +17,7 @@
 BF16 = jnp.bfloat16
 CHUNK_BLOCKS = 2
 NT = (((1,), (1,)), ((), ()))
+TN = (((0,), (0,)), ((), ()))
 
 
 def layer_norm(hidden, gain, shift):
@@ -115,58 +116,316 @@
     return owned
 
 
-def gather_vectors(vectors):
+def vector_kernel(number, at_ref, *refs):
+    rows, (vectors_ref, wide_ref, mix_ref, held) = refs[:-4], refs[-4:]
+    groups = len(rows)
+    for step in range(groups):
+        held[pl.ds(lax.rem(at_ref[1] + groups - step, groups), 1), :] = rows[step][...]
+    width = vectors_ref.shape[1] // groups
+    wide = wide_ref.shape[1] // groups
+    for group in range(groups):
+        for at in range(number):
+            part = held[group : group + 1, at * width : (at + 1) * width]
+            vectors_ref[at : at + 1, group * width : (group + 1) * width] = part
+        wide_ref[:, group * wide : (group + 1) * wide] = held[group : group + 1, number * width :]
+    model_width = vectors_ref.shape[1]
+    mix_ref[...] = jnp.zeros(mix_ref.shape, F32)
+    mix_ref[:, :model_width] = vectors_ref[0:1, :]
+    mix_ref[:, 2 * model_width :] = vectors_ref[1:2, :]
+
+
+def gather_vectors(vectors, wide, places):
     groups = lax.axis_size("fsdp")
-    own = lax.axis_index("fsdp")
-    packed = jnp.concatenate(vectors)[None]
-    whole = jnp.zeros((groups, packed.shape[1]), packed.dtype)
-    whole = lax.dynamic_update_slice(whole, packed, (own, 0))
-    for step in range(1, groups):
-        other = shift_fsdp(packed, step)
-        whole = lax.dynamic_update_slice(whole, other, ((own - step) % groups, 0))
-    gathered, at = [], 0
-    for vector in vectors:
-        width = vector.shape[0]
-        gathered.append(whole[:, at : at + width].reshape(-1).astype(F32))
-        at += width
-    return gathered
-
-
-def gather_weight_core(shard):
+    packed = jnp.concatenate(vectors + [wide])[None].astype(F32)
+    rows = [packed] + [shift_fsdp(packed, step) for step in range(1, groups)]
+    model_width, wide_width = groups * vectors[0].shape[0], groups * wide.shape[0]
+    vmem = pl.BlockSpec(memory_space=pltpu.VMEM)
+    return pl.pallas_call(
+        functools.partial(vector_kernel, len(vectors)),
+        in_specs=[pl.BlockSpec(memory_space=pltpu.SMEM)] + [vmem] * groups,
+        out_specs=[vmem] * 3,
+        out_shape=[
+            jax.ShapeDtypeStruct((len(vectors), model_width), F32),
+            jax.ShapeDtypeStruct((1, wide_width), F32),
+            jax.ShapeDtypeStruct((1, 3 * model_width), F32),
+        ],
+        scratch_shapes=[pltpu.VMEM((groups, packed.shape[1]), F32)],
+    )(places, *rows)
+
+
+def after(values, *signs):
+    return lax.optimization_barrier((values, signs))[0]
+
+
+def spread_chips(block):
+    found = {0: block}
+    for bit in range(2, lax.axis_size("ctx"), 2):
+        found[bit] = swap(block, bit)
+    return found
+
+
+def copy_kernel(plan, count, at_ref, *refs):
+    sources, targets = refs[:count], refs[count : count + 1]
+    slots, in_sems, out_sems = refs[count + 1 : -2], refs[-2], refs[-1]
+    arrivals = []
+    for at in range(count):
+        arrivals.append(pltpu.make_async_copy(sources[at], slots[at], in_sems.at[at]))
+        arrivals[at].start()
+    leaving = []
+    for at, moves in enumerate(plan(at_ref, slots, targets[0])):
+        arrivals[at].wait()
+        for source, target in moves:
+            leaving.append(pltpu.make_async_copy(source, target, out_sems.at[len(leaving)]))
+            leaving[-1].start()
+    for copy in leaving:
+        copy.wait()
+
+
+def assemble(places, sources, shape, plan, copies):
+    anywhere = pl.BlockSpec(memory_space=pl.ANY)
+    return pl.pallas_call(
+        functools.partial(copy_kernel, plan, len(sources)),
+        in_specs=[pl.BlockSpec(memory_space=pltpu.SMEM)] + [anywhere] * len(sources),
+        out_specs=anywhere,
+        out_shape=shape,
+        scratch_shapes=[pltpu.VMEM(source.shape, source.dtype) for source in sources]
+        + [pltpu.SemaphoreType.DMA((len(sources),)), pltpu.SemaphoreType.DMA((copies,))],
+        compiler_params=pltpu.CompilerParams(vmem_limit_bytes=32 * 1024 * 1024),
+        cost_estimate=pl.CostEstimate(flops=0, bytes_accessed=10_000_000, transcendentals=0),
+    )(places, *sources)
+
+
+def shift_all(piece):
+    return {step: shift_fsdp(piece, step) for step in range(1, lax.axis_size("fsdp"))}
+
+
+def row_of_step(own, step, rows):
+    groups = lax.axis_size("fsdp")
+    return pl.ds(lax.rem(own + groups - step, groups) * rows, rows)
+
+
+def halves_plan(rows, half):
+    groups = lax.axis_size("fsdp")
+
+    def plan(at_ref, slots, target):
+        own, core_at = at_ref[1], at_ref[0] & 1
+        moves = [[(slots[0], target.at[pl.ds(own * rows, rows)])]]
+        for at, side in ((1, core_at), (2, 1 - core_at)):
+            column = pl.ds(pl.multiple_of(side * half, 128), half)
+            moves.append(
+                [
+                    (slots[at].at[step - 1], target.at[row_of_step(own, step, rows), column])
+                    for step in range(1, groups)
+                ]
+            )
+        return moves
+
+    return plan
+
+
+def core_half(shard):
+    rows, columns = shard.shape
+    core = lax.axis_index("ctx") % 2
+    return lax.dynamic_slice(shard, (0, core * (columns // 2)), (rows, columns // 2))
+
+
+def stack_steps(fetched):
+    return jnp.stack([fetched[step] for step in sorted(fetched)])
+
+
+def whole_of_halves(shard, mine, theirs, places):
     rows, columns = shard.shape
     groups = lax.axis_size("fsdp")
-    own = lax.axis_index("fsdp")
-    core = lax.axis_index("ctx") % 2
-    halves = shard.reshape(2, rows // 2, columns)
-    whole = jnp.zeros((groups, 2, rows // 2, columns), shard.dtype)
-    whole = lax.dynamic_update_slice(whole, halves[None], (own, 0, 0, 0))
-    piece = lax.dynamic_index_in_dim(halves, core, 0, keepdims=False)
-    for step in range(1, groups):
-        piece = shift_fsdp(piece, 1)
-        at = (own - step) % groups
-        whole = lax.dynamic_update_slice(whole, piece[None, None], (at, core, 0, 0))
-        whole = lax.dynamic_update_slice(whole, swap(piece, 1)[None, None], (at, 1 - core, 0, 0))
-    return whole.reshape(groups * rows, columns)
-
-
-def gather_weight_ctx(shard):
+    shape = jax.ShapeDtypeStruct((groups * rows, columns), shard.dtype)
+    plan = halves_plan(rows, columns // 2)
+    return assemble(places, [shard, mine, theirs], shape, plan, 2 * groups - 1)
+
+
+def weight_by_core(shard, places):
+    piece = core_half(shard)
+    sign = yield piece
+    fetched = shift_all(piece)
+    if sign is not None:
+        fetched = after(fetched, sign)
+    mine = stack_steps(fetched)
+    yield whole_of_halves(shard, mine, swap(mine, 1), places)
+
+
+def two_weights_by_ctx(shard, second, places):
     rows, columns = shard.shape
     number, groups = lax.axis_size("ctx"), lax.axis_size("fsdp")
-    own, me = lax.axis_index("fsdp"), lax.axis_index("ctx")
-    chips = ctx_bits()
-    half = columns // 2
-    parts = shard.reshape(number, rows // number, columns)
-    whole = jnp.zeros((groups, number, rows // number, columns), shard.dtype)
-    whole = lax.dynamic_update_slice(whole, parts[None], (own, 0, 0, 0))
-    piece = lax.dynamic_index_in_dim(parts, me, 0, keepdims=False)
-    for step in range(1, groups):
-        piece = shift_fsdp(piece, 1)
-        at = (own - step) % groups
-        left_half = gather_ctx(piece[:, :half], chips + [1])
-        right_half = gather_ctx(piece[:, half:], chips[::-1] + [1])
-        whole = lax.dynamic_update_slice(whole, left_half[None], (at, 0, 0, 0))
-        whole = lax.dynamic_update_slice(whole, right_half[None], (at, 0, 0, half))
-    return whole.reshape(groups * rows, columns)
+    me = lax.axis_index("ctx")
+    width = columns // number
+    piece = lax.dynamic_slice(shard, (0, me * width), (rows, width))
+    pieces = jnp.stack([piece, core_half(second)])
+    sign = yield pieces
+    fetched = shift_all(pieces)
+    if sign is not None:
+        fetched = after(fetched, sign)
+    fetched = stack_steps(fetched)
+    stack, mine = fetched[:, 0], fetched[:, 1]
+    sign = yield stack
+    near = spread_chips(stack)
+    near_bits = sorted(near)
+    near_list = after([near[bit] for bit in near_bits], sign)
+    across = swap(jnp.stack(near_list + [mine]), 1)
+    yield across
+
+    def plan(at_ref, slots, target):
+        own, at = at_ref[1], at_ref[0]
+
+        def moves_of(slot, other):
+            column = pl.ds(pl.multiple_of(other * width, 128), width)
+            return [
+                (slot.at[step - 1], target.at[row_of_step(own, step, rows), column])
+                for step in range(1, groups)
+            ]
+
+        moves = [moves_of(slots[index], at ^ bit) for index, bit in enumerate(near_bits)]
+        last = []
+        for index, bit in enumerate(near_bits):
+            last += moves_of(slots[-2].at[index], at ^ bit ^ 1)
+        return moves + [last, [(slots[-1], target.at[pl.ds(own * rows, rows)])]]
+
+    shape = jax.ShapeDtypeStruct((groups * rows, columns), shard.dtype)
+    whole = assemble(
+        places, near_list + [across, shard], shape, plan, number * (groups - 1) + 1
+    )
+    yield whole, whole_of_halves(second, mine, across[-1], places)
+
+
+def stacked_pieces(grad, blocks):
+    groups, chips = lax.axis_size("fsdp"), lax.axis_size("ctx") // 2
+    rows, width = grad.shape[0], grad.shape[1] // blocks
+    parts = [
+        grad[:, at * width : (at + 1) * width].reshape(
+            groups, chips, 2, rows // (2 * groups * chips), width
+        )
+        for at in range(blocks)
+    ]
+    return jnp.concatenate(parts, axis=3)
+
+
+def pieces_of(grad, column_blocks):
+    groups, chips = lax.axis_size("fsdp"), lax.axis_size("ctx") // 2
+    rows, columns = grad.shape
+    if column_blocks < 0:
+        return stacked_pieces(grad, -column_blocks)
+    if column_blocks == 1:
+        return grad.reshape(groups, chips, 2, rows // (2 * groups * chips), columns)
+    width = columns // chips
+    viewed = jnp.stack([grad[:, at * width : (at + 1) * width] for at in range(chips)])
+    viewed = viewed.reshape(chips, groups, 2, rows // (2 * groups), width)
+    return jnp.swapaxes(viewed, 0, 1)
+
+
+VECTOR_ROWS = 8
+
+
+def finish_kernel(near_bits, parts, at_ref, *refs):
+    me = at_ref[0]
+    sources, outs = refs[: len(near_bits) + 1], refs[len(near_bits) + 1 :]
+
+    def put(values, other):
+        first = 0
+        for out_ref, (rows, column_blocks) in zip(outs, parts):
+            part = values[first : first + rows]
+            width = part.shape[1]
+            if column_blocks < 0:
+                each = rows // -column_blocks
+                row = pl.ds(pl.multiple_of(other * each, 8), each)
+                for at in range(-column_blocks):
+                    piece = part[at * each : (at + 1) * each]
+                    out_ref[row, at * width : (at + 1) * width] = piece
+            elif column_blocks == 1:
+                out_ref[pl.ds(pl.multiple_of(other * rows, 8), rows), :] = part
+            else:
+                row = pl.ds(pl.multiple_of((other & 1) * rows, 8), rows)
+                out_ref[row, pl.ds(pl.multiple_of((other >> 1) * width, 128), width)] = part
+            first += rows
+
+    for index, bit in enumerate(near_bits):
+        put(sources[index][...].astype(F32), me ^ bit)
+        put(sources[-1][index].astype(F32), me ^ bit ^ 1)
+
+
+def sum_pack(grads, blocks, vectors, places):
+    number, groups = lax.axis_size("ctx"), lax.axis_size("fsdp")
+    me, own = lax.axis_index("ctx"), lax.axis_index("fsdp")
+    core, chip, chips = me % 2, me // 2, number // 2
+    views = [pieces_of(grad, block) for grad, block in zip(grads, blocks)]
+    width = views[0].shape[4]
+    if vectors:
+        rows = [vector.reshape(groups, 1, -1) for vector in vectors]
+        rows = [jnp.pad(row, ((0, 0), (0, 0), (0, width - row.shape[2]))) for row in rows]
+        rows += [jnp.zeros_like(rows[0])] * (number - len(rows))
+        view = jnp.concatenate(rows, axis=1).astype(BF16)
+        view = view.reshape(groups, chips, 2, 1, width)
+        views.append(jnp.pad(view, ((0, 0), (0, 0), (0, 0), (0, VECTOR_ROWS - 1), (0, 0))))
+
+    def side(which):
+        parts = [
+            jnp.swapaxes(lax.dynamic_index_in_dim(view, which, 2, keepdims=False), 0, 1)
+            for view in views
+        ]
+        return jnp.concatenate(parts, axis=2) if len(parts) > 1 else parts[0]
+
+    send = side(1 - core)
+    sign = yield send
+    other = swap(send, 1)
+    if sign is not None:
+        other = after(other, sign)
+    held = (side(core).astype(F32) + other.astype(F32)).astype(BF16)
+
+    def chip_part(at):
+        return lax.dynamic_index_in_dim(held, at, 0, keepdims=False)
+
+    sends = [chip_part(chip ^ (bit // 2)) for bit in range(2, number, 2)]
+    sign = yield sends
+    others = [swap(send, bit) for send, bit in zip(sends, range(2, number, 2))]
+    if sign is not None:
+        others = after(others, sign)
+    total = chip_part(chip).astype(F32)
+    for other in others:
+        total = total + other.astype(F32)
+    piece = total.astype(BF16)
+    sends = [
+        lax.dynamic_index_in_dim(piece, (own + step) % groups, 0, keepdims=False)
+        for step in range(1, groups)
+    ]
+    sign = yield sends
+    others = [shift_fsdp(send, step) for send, step in zip(sends, range(1, groups))]
+    if sign is not None:
+        others = after(others, sign)
+    total = lax.dynamic_index_in_dim(piece, own, 0, keepdims=False).astype(F32)
+    for other in others:
+        total = total + other.astype(F32)
+    total = total.astype(BF16)
+    yield total
+    near = spread_chips(total)
+    near_bits = sorted(near)
+    stack = jnp.stack([near[bit] for bit in near_bits])
+    yield stack
+    across = swap(stack, 1)
+    parts = [(view.shape[3], block) for view, block in zip(views, list(blocks) + [1])]
+    shapes = [
+        jax.ShapeDtypeStruct((grad.shape[0] // groups, grad.shape[1]), F32) for grad in grads
+    ]
+    if vectors:
+        shapes.append(jax.ShapeDtypeStruct((number * VECTOR_ROWS, width), F32))
+    vmem = pl.BlockSpec(memory_space=pltpu.VMEM)
+    sums = pl.pallas_call(
+        functools.partial(finish_kernel, near_bits, parts),
+        in_specs=[pl.BlockSpec(memory_space=pltpu.SMEM)] + [vmem] * (len(near_bits) + 1),
+        out_specs=[vmem] * len(shapes),
+        out_shape=shapes,
+        compiler_params=pltpu.CompilerParams(vmem_limit_bytes=32 * 1024 * 1024),
+    )(places, *[near[bit] for bit in near_bits], across)
+    owned = [
+        sums[-1][at * VECTOR_ROWS, : vector.shape[0] // groups]
+        for at, vector in enumerate(vectors)
+    ]
+    yield list(sums[: len(grads)]), owned
 
 
 def head_masks(rows):
@@ -345,21 +604,80 @@
     )(place, *operands)
 
 
-def mix_specs(number, tokens, pairs):
+def mix_specs(number, seq, tokens, pairs):
     def own(part):
-        return pl.BlockSpec((1, tokens, PAIR), lambda h, place: (place[0], 0, part * pairs + h))
+        return pl.BlockSpec(
+            (1, None, tokens, PAIR), lambda h, place: (place[0], seq, 0, part * pairs + h)
+        )
 
     def every(part):
-        return pl.BlockSpec((number, tokens, PAIR), lambda h, place: (0, 0, part * pairs + h))
+        return pl.BlockSpec(
+            (number, None, tokens, PAIR), lambda h, place: (0, seq, 0, part * pairs + h)
+        )
 
     return own, every
 
 
-def attend_forward(place, mix):
-    number, tokens, width = mix.shape
+def mix_kernel(x_ref, weight_ref, add_ref, out_ref):
+    for at in range(x_ref.shape[0]):
+        mixed = jnp.dot(x_ref[at], weight_ref[...], preferred_element_type=F32)
+        out_ref[at] = (mixed + add_ref[...]).astype(BF16)
+
+
+def mix_tokens(tokens_all, weight, add):
+    number, seqs, tokens, model_width = tokens_all.shape
+    width = weight.shape[1]
+    return pl.pallas_call(
+        mix_kernel,
+        grid=(number,),
+        in_specs=[
+            pl.BlockSpec((None, seqs, tokens, model_width), lambda at: (at, 0, 0, 0)),
+            pl.BlockSpec((model_width, width), lambda at: (0, 0)),
+            pl.BlockSpec((1, width), lambda at: (0, 0)),
+        ],
+        out_specs=pl.BlockSpec((None, seqs, tokens, width), lambda at: (at, 0, 0, 0)),
+        out_shape=jax.ShapeDtypeStruct((number, seqs, tokens, width), BF16),
+        compiler_params=pltpu.CompilerParams(vmem_limit_bytes=48 * 1024 * 1024),
+        cost_estimate=pl.CostEstimate(
+            flops=2 * number * seqs * tokens * model_width * width,
+            bytes_accessed=2 * number * seqs * tokens * (model_width + width),
+            transcendentals=0,
+        ),
+    )(tokens_all, weight, add)
+
+
+def outer_kernel(left_ref, right_ref, out_ref):
+    out_ref[...] = lax.dot_general(
+        left_ref[...], right_ref[...], TN, preferred_element_type=F32
+    ).astype(BF16)
+
+
+def outer_products(left, parts):
+    rows, model_width = left.shape
+    number, _, columns = parts.shape
+    return pl.pallas_call(
+        outer_kernel,
+        grid=(number,),
+        in_specs=[
+            pl.BlockSpec((rows, model_width), lambda at: (0, 0)),
+            pl.BlockSpec((None, rows, columns), lambda at: (at, 0, 0)),
+        ],
+        out_specs=pl.BlockSpec((model_width, columns), lambda at: (0, at)),
+        out_shape=jax.ShapeDtypeStruct((model_width, number * columns), BF16),
+        compiler_params=pltpu.CompilerParams(vmem_limit_bytes=48 * 1024 * 1024),
+        cost_estimate=pl.CostEstimate(
+            flops=2 * model_width * rows * number * columns,
+            bytes_accessed=6_000_000,
+            transcendentals=0,
+        ),
+    )(left, parts)
+
+
+def attend_forward(place, seq, mix):
+    number, _, tokens, width = mix.shape
     model_width = width // 3
     pairs = model_width // PAIR
-    own, every = mix_specs(number, tokens, pairs)
+    own, every = mix_specs(number, seq, tokens, pairs)
     chunk = CHUNK_BLOCKS * tokens
     block = pl.BlockSpec((tokens, PAIR), lambda h, place: (0, h))
     return kernel_call(
@@ -376,15 +694,15 @@
         (block, block, block, pl.BlockSpec((1, 2, tokens), lambda h, place: (h, 0, 0))),
         pairs,
         [pltpu.VMEM((2, number // CHUNK_BLOCKS, tokens, chunk), F32)],
-        8 * number * tokens * tokens * model_width,
-    )
-
-
-def attend_queries(place, mix, grads, attended, column):
-    number, tokens, width = mix.shape
+        56 * number * tokens * tokens * model_width,
+    )
+
+
+def attend_queries(place, seq, mix, grads, attended, column):
+    number, _, tokens, width = mix.shape
     model_width = width // 3
     pairs = model_width // PAIR
-    own, every = mix_specs(number, tokens, pairs)
+    own, every = mix_specs(number, seq, tokens, pairs)
     block = pl.BlockSpec((tokens, PAIR), lambda h, place: (0, h))
     return kernel_call(
         query_kernel,
@@ -395,15 +713,15 @@
         block,
         pairs,
         [],
-        12 * number * tokens * tokens * model_width,
-    )
-
-
-def attend_keys(place, mix, all_grads, stats):
-    number, tokens, width = mix.shape
+        56 * number * tokens * tokens * model_width,
+    )
+
+
+def attend_keys(place, seq, mix, all_grads, stats):
+    number, _, tokens, width = mix.shape
     model_width = width // 3
     pairs = model_width // PAIR
-    own, every = mix_specs(number, tokens, pairs)
+    own, every = mix_specs(number, seq, tokens, pairs)
     block = pl.BlockSpec((tokens, PAIR), lambda h, place: (0, h))
     return kernel_call(
         key_kernel,
@@ -413,8 +731,8 @@
             own(1),
             own(2),
             every(0),
-            every(0),
-            pl.BlockSpec((number, 1, 4, tokens), lambda h, place: (0, h, 0, 0)),
+            pl.BlockSpec((number, None, tokens, PAIR), lambda h, place: (0, seq, 0, h)),
+            pl.BlockSpec((number, None, 1, 4, tokens), lambda h, place: (0, seq, h, 0, 0)),
         ],
         (
             jax.ShapeDtypeStruct((tokens, model_width), BF16),
@@ -423,7 +741,7 @@
         (block, block),
         pairs,
         [],
-        16 * number * tokens * tokens * model_width,
+        72 * number * tokens * tokens * model_width,
     )
 
 
@@ -451,56 +769,68 @@
     number = lax.axis_size("ctx")
     pairs = model_width // PAIR
     me = lax.axis_index("ctx")
-    chips = ctx_bits()
-    orders = (chips + [1], chips[::-1] + [1])
-
-    def gather_tokens(blocked):
-        return [gather_ctx(blocked[at], orders[at % 2]) for at in range(seq_count)]
-
-    tokens_all = gather_tokens(hidden_states)
-    attend_full = gather_weight_core(attend_weight)
-    (
-        query_add,
-        value_add,
-        output_add,
-        gain_first,
-        shift_first,
-        raise_add,
-        lower_add,
-        gain_second,
-        shift_second,
-    ) = gather_vectors(
+    places = jnp.stack([me, lax.axis_index("fsdp")]).astype(jnp.int32)
+
+    tokens_all = lax.all_gather(hidden_states, "ctx", axis=0, tiled=False)
+    attend_stages = weight_by_core(attend_weight, places)
+    attend_piece = next(attend_stages)
+    attend_full = attend_stages.send(None)
+    attend_sign = attend_full
+    packed = (raise_weight.shape[1] // number) == output_weight.shape[1] // 2
+    vectors = after(
         [
             query_bias,
             value_bias,
             output_bias,
             first_gain,
             first_shift,
-            raise_bias,
             lower_bias,
             second_gain,
             second_shift,
-        ]
-    )
-    output_full = gather_weight_core(output_weight)
-    raise_full = gather_weight_ctx(raise_weight)
-    lower_full = gather_weight_ctx(lower_weight)
-
-    mix_add = jnp.concatenate([query_add, jnp.zeros_like(query_add), value_add])
-    places = [
+        ],
+        attend_piece,
+    )
+    vector_rows, raise_add, mix_add = gather_vectors(vectors, raise_bias, places)
+    output_add, gain_first, shift_first, lower_add, gain_second, shift_second = [
+        vector_rows[at : at + 1] for at in range(2, 8)
+    ]
+    if packed:
+        raise_stages = two_weights_by_ctx(
+            after(raise_weight, attend_sign), output_weight, places
+        )
+        raise_sign = next(raise_stages)
+        lower_stages = weight_by_core(after(lower_weight, raise_sign), places)
+        tokens_all = after(tokens_all, raise_sign)
+        lower_sign = next(lower_stages)
+    else:
+        raise_stages = weight_by_core(raise_weight, places)
+        output_stages = weight_by_core(output_weight, places)
+        lower_stages = weight_by_core(lower_weight, places)
+        next(lower_stages)
+        next(raise_stages)
+        next(output_stages)
+
+    seq_places = [
         jnp.stack([me.astype(jnp.int32), lengths[at].astype(jnp.int32)]) for at in range(seq_count)
     ]
-    mixes = []
+    mix = mix_tokens(tokens_all, attend_full, mix_add)
+    attended, attended_lows, columns, lse_rows = [], [], [], []
     for at in range(seq_count):
-        mixed = jnp.dot(
-            tokens_all[at].reshape(number * tok_count, model_width),
-            attend_full,
-            preferred_element_type=F32,
-        )
-        mixes.append((mixed + mix_add).astype(BF16).reshape(number, tok_count, 3 * model_width))
-    attended, attended_lows, columns, lse_rows = zip(
-        *[attend_forward(places[at], mixes[at]) for at in range(seq_count)]
-    )
+        if packed and at == 0:
+            raise_sign = raise_stages.send(mix)
+            mix = after(mix, raise_sign, lower_sign)
+        if packed and at == 1:
+            raise_sign = raise_stages.send(attended_lows[0])
+            mix = after(mix, raise_sign)
+        one, low, column, lse_row = attend_forward(seq_places[at], at, mix)
+        attended.append(one)
+        attended_lows.append(low)
+        columns.append(column)
+        lse_rows.append(lse_row)
+    if packed:
+        raise_full, output_full = next(raise_stages)
+    else:
+        raise_full, output_full = raise_stages.send(None), output_stages.send(None)
     attended_low = jnp.concatenate(attended_lows, axis=0)
 
     token_rows = hidden_states.reshape(row_count, model_width)
@@ -512,38 +842,44 @@
     raised = jnp.dot(first_low, raise_full, preferred_element_type=F32) + raise_add
     active, gelu_back = jax.vjp(gelu_exact, raised)
     active_low = active.astype(BF16)
+    lower_full = lower_stages.send(first_low)
     lowered = jnp.dot(active_low, lower_full, preferred_element_type=F32) + lower_add
     result, second_back = jax.vjp(layer_norm, normed_first + lowered, gain_second, shift_second)
     layer_output = result.astype(BF16).reshape(block_shape)
     grad_out = cotangent.reshape(row_count, model_width).astype(F32)
     grad_mid, grad_gain_second, grad_shift_second = second_back(grad_out)
+    grad_gain_second, grad_shift_second = grad_gain_second[0], grad_shift_second[0]
     mid_low = grad_mid.astype(BF16)
-    grad_lower_weight = jnp.einsum("rf,rd->fd", active_low, mid_low, preferred_element_type=F32)
+    shared = model_width % (8 * number * lax.axis_size("fsdp")) == 0
+    grad_lower_weight = jnp.einsum("rf,rd->fd", active_low, mid_low, preferred_element_type=F32).astype(BF16)
+    if shared:
+        lower_pack = sum_pack([grad_lower_weight], [1], [], places)
+        mid_low = after(mid_low, next(lower_pack))
     grad_lower_add = jnp.sum(mid_low.astype(F32), axis=0)
     grad_active = jnp.einsum("rd,fd->rf", mid_low, lower_full, preferred_element_type=F32)
     (grad_raised,) = gelu_back(grad_active)
     raised_low = grad_raised.astype(BF16)
-    grad_raise_weight = jnp.einsum("rd,rf->df", first_low, raised_low, preferred_element_type=F32)
+    grad_raise_weight = jnp.einsum("rd,rf->df", first_low, raised_low, preferred_element_type=F32).astype(BF16)
     grad_raise_add = jnp.sum(raised_low.astype(F32), axis=0)
     grad_first = grad_mid + jnp.einsum(
         "rf,df->rd", raised_low, raise_full, preferred_element_type=F32
     )
     grad_resid, grad_gain_first, grad_shift_first = first_back(grad_first)
+    grad_gain_first, grad_shift_first = grad_gain_first[0], grad_shift_first[0]
     resid_low = grad_resid.astype(BF16)
     grad_output_weight = jnp.einsum(
         "rc,rd->cd", attended_low, resid_low, preferred_element_type=F32
-    )
+    ).astype(BF16)
     grad_output_add = jnp.sum(resid_low.astype(F32), axis=0)
     grad_att = (
         jnp.einsum("rd,cd->rc", resid_low, output_full, preferred_element_type=F32)
         .astype(BF16)
         .reshape(block_shape)
     )
-    grads_all = gather_tokens(grad_att)
+    grads_all = lax.all_gather(grad_att, "ctx", axis=0, tiled=False)
     head_of = lax.broadcasted_iota(jnp.int32, (HEADS, model_width), 1) // HEAD_DIM
     pick = (head_of == lax.broadcasted_iota(jnp.int32, (HEADS, model_width), 0)).astype(F32)
-    query_grads, key_grads, value_grads = [], [], []
-    stats_all = []
+    stats = []
     for at in range(seq_count):
         delta = jnp.einsum(
             "hd,td->ht",
@@ -552,29 +888,70 @@
             precision=lax.Precision.HIGHEST,
             preferred_element_type=F32,
         ).reshape(pairs, 2, tok_count)
-        stats_all.append(
-            gather_ctx(jnp.concatenate([lse_rows[at], delta], axis=1), orders[at % 2])
+        stats.append(jnp.concatenate([lse_rows[at], delta], axis=1))
+    stats = jnp.stack(stats)
+    stats_all = lax.all_gather(stats, "ctx", axis=0, tiled=False)
+    early = [
+        grad_output_add,
+        grad_gain_first,
+        grad_shift_first,
+        grad_raise_add,
+        grad_lower_add,
+        grad_gain_second,
+        grad_shift_second,
+    ]
+    query_grads, key_grads, value_grads = [], [], []
+    if shared:
+        raise_pack = sum_pack(
+            [grad_raise_weight, grad_output_weight], [number // 2, 1], early, places
         )
+        mix = after(mix, lower_pack.send(grad_att), next(raise_pack))
     for at in range(seq_count):
         query_grads.append(
-            attend_queries(places[at], mixes[at], grad_att[at], attended[at], columns[at])
+            attend_queries(seq_places[at], at, mix, grad_att[at], attended[at], columns[at])
         )
+        if shared and at == 0:
+            mix = after(mix, raise_pack.send(query_grads[0]))
+    if shared:
+        mix = after(mix, lower_pack.send(query_grads[-1]))
     for at in range(seq_count):
-        grad_keys, grad_values = attend_keys(places[at], mixes[at], grads_all[at], stats_all[at])
+        grad_keys, grad_values = attend_keys(seq_places[at], at, mix, grads_all, stats_all)
         key_grads.append(grad_keys)
         value_grads.append(grad_values)
+        if shared and at == 0:
+            mix = after(mix, raise_pack.send(grad_keys), lower_pack.send(grad_keys))
+    if shared:
+        value_grads[-1] = after(
+            value_grads[-1], raise_pack.send(value_grads[-1]), next(lower_pack)
+        )
     query_low = jnp.concatenate(query_grads, axis=0)
     key_low = jnp.concatenate(key_grads, axis=0)
     value_low = jnp.concatenate(value_grads, axis=0)
     grad_mixture = jnp.concatenate([query_low, key_low, value_low], axis=1)
-    grad_attend_weight = jnp.einsum(
-        "rd,rc->dc", token_rows, grad_mixture, preferred_element_type=F32
+    grad_attend_weight = outer_products(
+        token_rows, jnp.stack([query_low, key_low, value_low])
     )
     grad_query_add = jnp.sum(query_low.astype(F32), axis=0)
     grad_value_add = jnp.sum(value_low.astype(F32), axis=0)
     hidden_grad = grad_resid + jnp.einsum(
         "rc,dc->rd", grad_mixture, attend_full, preferred_element_type=F32
     )
+    late = [grad_query_add, grad_value_add]
+    if shared:
+        attend_pack = sum_pack([grad_attend_weight], [-3], late, places)
+        next(attend_pack)
+        for _ in range(4):
+            attend_pack.send(None)
+        (grad_attend_weight,), late = next(attend_pack)
+        next(raise_pack)
+        (grad_lower_weight,), _ = next(lower_pack)
+        (grad_raise_weight, grad_output_weight), early = next(raise_pack)
+    else:
+        grad_lower_weight = sum_weight(grad_lower_weight)
+        grad_raise_weight = sum_weight(grad_raise_weight)
+        grad_output_weight = sum_weight(grad_output_weight)
+        grad_attend_weight = sum_weight(grad_attend_weight)
+        early, late = sum_vectors(early), sum_vectors(late)
     (
         grad_output_add,
         grad_gain_first,
@@ -583,31 +960,21 @@
         grad_lower_add,
         grad_gain_second,
         grad_shift_second,
-    ) = sum_vectors(
-        [
-            grad_output_add,
-            grad_gain_first,
-            grad_shift_first,
-            grad_raise_add,
-            grad_lower_add,
-            grad_gain_second,
-            grad_shift_second,
-        ]
-    )
-    grad_query_add, grad_value_add = sum_vectors([grad_query_add, grad_value_add])
+    ) = early
+    grad_query_add, grad_value_add = late
     return (
         layer_output,
         hidden_grad.reshape(block_shape),
-        sum_weight(grad_attend_weight),
+        grad_attend_weight,
         grad_query_add,
         grad_value_add,
-        sum_weight(grad_output_weight),
+        grad_output_weight,
         grad_output_add,
         grad_gain_first,
         grad_shift_first,
-        sum_weight(grad_raise_weight),
+        grad_raise_weight,
         grad_raise_add,
-        sum_weight(grad_lower_weight),
+        grad_lower_weight,
         grad_lower_add,
         grad_gain_second,
         grad_shift_second,

time: 674 us -> 486 us (0.72)
  waiting for transfers between devices: 229 us -> 103 us
  local copies, waits for them, and re-layouts: 70.6 us -> 38.8 us
  matrix products: 78.9 us -> 51.1 us
  starting transfers between devices: 104 us -> 78.9 us
  Pallas kernels: 136 us -> 159 us
  other arithmetic: 43.2 us -> 24.9 us
  between operations: 3.62 us -> 15.7 us
  blocking collectives: 0 us -> 9.54 us
    ppermute x110 -> x30, waiting for transfers between devices: 145 us -> 35.4 us  [swap(): return lax.ppermute(value, 'ctx', [(at, at ^ bit) for at in range(number)])]
    ppermute x110 -> x30, starting transfers between devices: 75.7 us -> 24.9 us  [swap(): return lax.ppermute(value, 'ctx', [(at, at ^ bit) for at in range(number)])]
    pallas_call x0 -> x10, Pallas kernels: none -> 39.2 us  [the longest x1 18.9 us: mix_tokens(): pl.pallas_call(mix_kernel, grid=(number,), in_specs=[pl.BlockSpec((None,...]
    ppermute x33 -> x21, starting transfers between devices: 28.2 us -> 53.9 us  [shift_fsdp(): lax.ppermute(value, 'fsdp', [(at, (at + step) % number) for at in range(n...]
    dot_general x3 -> x0, matrix products: 21.5 us -> none  [the longest x2 19.5 us: on_device(): jnp.dot(tokens_all[at].reshape(number * tok_count, model_width), attend_f...]
    dynamic_update_slice x32 -> x0, local copies, waits for them, and re-layouts: 18 us -> none  [the longest x6 5.57 us: gather_weight_ctx(): whole = lax.dynamic_update_slice(whole, right_half[None], (at, 0, 0, half))]
    ppermute x33 -> x21, waiting for transfers between devices: 84.4 us -> 67.2 us  [shift_fsdp(): lax.ppermute(value, 'fsdp', [(at, (at + step) % number) for at in range(n...]
    pallas_call x6, Pallas kernels: 136 us -> 120 us  [kernel_call(): pl.pallas_call(body, grid_spec=pltpu.PrefetchScalarGridSpec(num_scalar_pr...]
  transfers between devices with their start and end apart: 143 -> 53, of which waited for: 76 -> 14; matrix products, arithmetic and copies ran while one was open for 16% -> 14% of each run, Pallas kernels for 17% -> 31%
where the time goes in v2:
time: 486 us; the launch traced here: 481 us
  Pallas kernels  159 us (33%)
  waiting for transfers between devices  103 us (21%)
  starting transfers between devices  78.9 us (16%)
  matrix products  51.1 us (11%)
  local copies, waits for them, and re-layouts  38.8 us (8%)
  other arithmetic  24.9 us (5%)
  between operations  15.7 us (3%)
  blocking collectives  9.54 us (2%)
    pallas_call x6, Pallas kernels, kernel_call(): pl.pallas_call(body, grid_spec=pltpu.PrefetchScalarGridSpec(num_scalar_pr...  120 us
    ppermute x21, waiting for transfers between devices, shift_fsdp(): lax.ppermute(value, 'fsdp', [(at, (at + step) % number) for at in range(n...  67.2 us
    ppermute x21, starting transfers between devices, shift_fsdp(): lax.ppermute(value, 'fsdp', [(at, (at + step) % number) for at in range(n...  53.9 us
    ppermute x30, waiting for transfers between devices, swap(): return lax.ppermute(value, 'ctx', [(at, at ^ bit) for at in range(number)])  35.4 us
    ppermute x30, starting transfers between devices, swap(): return lax.ppermute(value, 'ctx', [(at, at ^ bit) for at in range(number)])  24.9 us
    pallas_call x1, Pallas kernels, mix_tokens(): pl.pallas_call(mix_kernel, grid=(number,), in_specs=[pl.BlockSpec((None,...  18.9 us
    dot_general x1, matrix products, on_device(): jnp.dot(first_low, raise_full, preferred_element_type=F32) + raise_add  18.4 us
    unnamed x137, local copies, waits for them, and re-layouts  13.5 us
  transfers between devices with their start and end apart: 53, of which 14 were waited for; matrix products, arithmetic and copies ran while one was open for 14% of the time, Pallas kernels for 31%

profile of v2, /device:TPU:0, one launch (start us, length us, event | category | flops | bytes accessed | tf_op | source)
XLA Modules:
  0.0 481.1 jit_solution(14197503244633919307)
XLA Ops:
  9.2 5.1 %collective-permute-start.2 = (bf16[192,1152]{1,0:T(8,128)(2,1)S(1)}, bf16[192,1152]{1,0:T(8,128)(2,1)S(1)}, u32[]{:S(2)}, u32[]{:S(2)}) collective-permute-start(bf16[192,1152]{1,0:T(8,128)(2,1)S(1)} %constant_dynamic-slice_fusion.7), channel_id=1, source_target_pairs={{0,3},{1,0},{2,1},{3,2},{4,7},{5,4},{6,5},{7,6},{8,11},{9,8},{10,9... | collective-permute-start | bytes 1327112 | tf_op jit(solution)/shard_map/ppermute | solution.py:41
  15.3 9.6 %collective-permute-done.2 = bf16[192,1152]{1,0:T(8,128)(2,1)S(1)} collective-permute-done((bf16[192,1152]{1,0:T(8,128)(2,1)S(1)}, bf16[192,1152]{1,0:T(8,128)(2,1)S(1)}, u32[]{:S(2)}, u32[]{:S(2)}) %collective-permute-start.2) | collective-permute-done | bytes 442400 | tf_op jit(solution)/shard_map/ppermute | solution.py:41
  24.9 27.1 %collective-permute-done.1 = bf16[192,1152]{1,0:T(8,128)(2,1)S(1)} collective-permute-done((bf16[192,1152]{1,0:T(8,128)(2,1)S(1)}, bf16[192,1152]{1,0:T(8,128)(2,1)S(1)}, u32[]{:S(2)}, u32[]{:S(2)}) %collective-permute-start.1) | collective-permute-done | bytes 442400 | tf_op jit(solution)/shard_map/ppermute | solution.py:41
  61.2 2.9 collective-permute-start.6
  81.8 18.9 %shard_map.273.q_ref.k_ref.v_ref = bf16[8,2,256,2304]{3,2,1,0:T(8,128)(2,1)} custom-call(bf16[8,2,256,768]{3,2,1,0:T(8,128)(2,1)} %bitcast.289, bf16[768,2304]{1,0:T(8,128)(2,1)S(1)} %copy-done.1, f32[1,2304]{1,0:T(1,128)S(1)} %copy-done.27), custom_call_target="tpu_custom_call" | custom-call | flops 14495514624 | bytes 25165824 | tf_op jit(solution)/shard_map/pallas_call | solution.py:630
  104.5 21.7 %shard_map.274 = (f32[256,768]{1,0:T(8,128)S(1)}, bf16[256,768]{1,0:T(8,128)(2,1)S(1)}, f32[256,768]{1,0:T(8,128)S(1)}, f32[6,2,256]{2,1,0:T(2,128)S(1)}) custom-call(s32[2]{0:T(128)S(1)} %copy-done.25, bf16[8,2,256,2304]{3,2,1,0:T(8,128)(2,1)} %shard_map.273.q_ref.k_ref.v_ref, bf16[8,2,256,2304]{3,2,1,0:T(8,128)(2,1)} %shard_map.273.q_ref.k_ref.v_ref, ...), custom_call_target="tpu_custom_call" | custom-call | flops 22548578304 | bytes 10000000 | tf_op jit(solution)/shard_map/pallas_call | solution.py:592
  131.8 3.5 collective-permute-start.14
  139.0 13.4 %shard_map.275 = (f32[256,768]{1,0:T(8,128)S(1)}, bf16[256,768]{1,0:T(8,128)(2,1)S(1)}, f32[256,768]{1,0:T(8,128)S(1)}, f32[6,2,256]{2,1,0:T(2,128)S(1)}) custom-call(s32[2]{0:T(128)S(1)} %get-tuple-element.223.place_ref, bf16[8,2,256,2304]{3,2,1,0:T(8,128)(2,1)} %shard_map.273.q_ref.k_ref.v_ref, bf16[8,2,256,2304]{3,2,1,0:T(8,128)(2,1)} %shard_map.273.q_ref.k_ref.v_ref, ...), custom_call_target="tpu_custom_call" | custom-call | flops 22548578304 | bytes 10000000 | tf_op jit(solution)/shard_map/pallas_call | solution.py:592
  155.8 19.1 %collective-permute-done.15 = bf16[768,384]{1,0:T(8,128)(2,1)S(1)} collective-permute-done((bf16[768,384]{1,0:T(8,128)(2,1)}, bf16[768,384]{1,0:T(8,128)(2,1)S(1)}, u32[]{:S(2)}, u32[]{:S(2)}) %collective-permute-start.15) | collective-permute-done | bytes 589856 | tf_op jit(solution)/shard_map/ppermute | solution.py:41
  175.3 3.3 shard_map.277
  178.6 18.4 %multiply_convert_fusion = (bf16[512,3072]{1,0:T(8,128)(2,1)S(1)}, f32[512,3072]{1,0:T(8,128)}, f32[512,3072]{1,0:T(8,128)}) fusion(f32[3072]{0:T(1024)S(1)} %bitcast.290, bf16[512,768]{1,0:T(8,128)(2,1)S(1)} %fusion.25, bf16[768,3072]{1,0:T(8,128)(2,1)S(1)} %shard_map.277), kind=kOutput, calls=%fused_computation.4 | convolution fusion | flops 2519728128 | bytes 21245952 | tf_op jit(solution)/shard_map/dot_general | solution.py:842
  204.9 3.5 convolution_convert_fusion.1
  211.7 8.7 %fusion.66 = (bf16[3072]{0:T(1024)(128)(2,1)S(1)}, bf16[512,3072]{1,0:T(8,128)(2,1)}) fusion(f32[512,3072]{1,0:T(8,128)} %get-tuple-element.159, f32[512,3072]{1,0:T(8,128)} %get-tuple-element.218, f32[3072]{0:T(1024)S(1)} %bitcast.291, bf16[512,768]{1,0:T(8,128)(2,1)S(1)} %add_convert_fusion.5, bf16[3072,768]{1,0:T(8,128)(2,1)S(1)} %shard_map.278), kind=kOutput, calls=%fused_computation.212 | convolution fusion | flops 2441081856 | bytes 21252096 | tf_op jit(solution)/shard_map/rd,fd->rf/dot_general | solution.py:859
  220.4 5.0 %multiply_reduce_fusion = (bf16[768]{0:T(1024)(128)(2,1)S(1)}, f32[512]{0:T(512)S(1)}, bf16[768]{0:T(1024)(128)(2,1)S(1)}, f32[512,768]{1,0:T(8,128)S(1)}) fusion(f32[512,768]{1,0:T(8,128)S(1)} %get-tuple-element.217, f32[512]{0:T(512)S(1)} %fusion.61, f32[512]{0:T(512)S(1)} %broadcast_multiply_fusion.1, f32[768]{0:T(1024)S(1)} %get-tuple-element.148, ...), kind=kOutput, calls=%fused_computation.56 | convolution fusion | flops 2419849216 | bytes 12597248 | tf_op jit(solution)/shard_map/rf,df->rd/dot_general | solution.py:864
  241.9 3.1 fusion.7
  248.7 22.2 %shard_map.279 = bf16[256,768]{1,0:T(8,128)(2,1)S(1)} custom-call(s32[2]{0:T(128)S(1)} %copy-done.26, bf16[8,2,256,2304]{3,2,1,0:T(8,128)(2,1)} %shard_map.273.q_ref.k_ref.v_ref, bf16[8,2,256,2304]{3,2,1,0:T(8,128)(2,1)} %shard_map.273.q_ref.k_ref.v_ref, bf16[8,2,256,2304]{3,2,1,0:T(8,128)(2,1)} %shard_map.273.q_ref.k_ref.v_ref, ...), custom_call_target="tpu_custom_call" | custom-call | flops 22548578304 | bytes 10000000 | tf_op jit(solution)/shard_map/pallas_call | solution.py:592
  276.3 12.6 %shard_map.280 = bf16[256,768]{1,0:T(8,128)(2,1)S(1)} custom-call(s32[2]{0:T(128)S(1)} %get-tuple-element.223.place_ref, bf16[8,2,256,2304]{3,2,1,0:T(8,128)(2,1)} %shard_map.273.q_ref.k_ref.v_ref, bf16[8,2,256,2304]{3,2,1,0:T(8,128)(2,1)} %shard_map.273.q_ref.k_ref.v_ref, bf16[8,2,256,2304]{3,2,1,0:T(8,128)(2,1)} %shard_map.273.q_ref.k_ref.v_ref, ...), custom_call_target="tpu_custom_call" | custom-call | flops 22548578304 | bytes 10000000 | tf_op jit(solution)/shard_map/pallas_call | solution.py:592
  288.9 3.1 collective-permute-done.22
  293.1 9.3 %collective-permute-start.26 = (bf16[96,768]{1,0:T(8,128)(2,1)}, bf16[96,768]{1,0:T(8,128)(2,1)}, u32[]{:S(2)}, u32[]{:S(2)}) collective-permute-start(bf16[96,768]{1,0:T(8,128)(2,1)} %get-tuple-element.194), channel_id=1, source_target_pairs={{0,1},{1,2},{2,3},{3,0},{4,5},{5,6},{6,7},{7,4},{8,9},{9,10},{10,1... | collective-permute-start | bytes 442376 | tf_op jit(solution)/shard_map/ppermute | solution.py:41
  302.4 9.5 %all-gather.1 = f32[16,6,4,256]{3,2,1,0:T(4,128)S(1)} all-gather(f32[2,6,4,256]{3,2,1,0:T(4,128)S(1)} %pad_maximum_fusion.12), channel_id=3, replica_groups=mesh['ctx'=8,'fsdp'=4] {'ctx'}, dimensions={0}, use_global_device_ids=true | all-gather | bytes 442368 | tf_op jit(solution)/shard_map/all_gather | solution.py:893
  315.7 6.8 %collective-permute-start.27 = (bf16[96,768]{1,0:T(8,128)(2,1)}, bf16[96,768]{1,0:T(8,128)(2,1)}, u32[]{:S(2)}, u32[]{:S(2)}) collective-permute-start(bf16[96,768]{1,0:T(8,128)(2,1)} %get-tuple-element.193), channel_id=1, source_target_pairs={{0,2},{1,3},{2,0},{3,1},{4,6},{5,7},{6,4},{7,5},{8,10},{9,11},{10,... | collective-permute-start | bytes 442376 | tf_op jit(solution)/shard_map/ppermute | solution.py:41
  322.8 24.8 %shard_map.281 = (bf16[256,768]{1,0:T(8,128)(2,1)S(1)}, bf16[256,768]{1,0:T(8,128)(2,1)S(1)}) custom-call(s32[2]{0:T(128)S(1)} %copy-done.26, bf16[8,2,256,2304]{3,2,1,0:T(8,128)(2,1)} %shard_map.273.q_ref.k_ref.v_ref, bf16[8,2,256,2304]{3,2,1,0:T(8,128)(2,1)} %shard_map.273.q_ref.k_ref.v_ref, bf16[8,2,256,2304]{3,2,1,0:T(8,128)(2,1)} %shard_map.273.q_ref.k_ref.v_ref, ...), custom_call_target="tpu_custom_call" | custom-call | flops 28991029248 | bytes 10000000 | tf_op jit(solution)/shard_map/pallas_call | solution.py:592
  356.4 5.9 %collective-permute-start.30 = (bf16[128,768]{1,0:T(8,128)(2,1)S(1)}, bf16[128,768]{1,0:T(8,128)(2,1)S(1)}, u32[]{:S(2)}, u32[]{:S(2)}) collective-permute-start(bf16[128,768]{1,0:T(8,128)(2,1)S(1)} %get-tuple-element.188), channel_id=1, source_target_pairs={{0,2},{1,3},{2,0},{3,1},{4,6},{5,7},{6,4},{7,5},{8,10},{9,11},{10,... | collective-permute-start | bytes 589832 | tf_op jit(solution)/shard_map/ppermute | solution.py:41
  362.4 24.8 %shard_map.282 = (bf16[256,768]{1,0:T(8,128)(2,1)S(1)}, bf16[256,768]{1,0:T(8,128)(2,1)S(1)}) custom-call(s32[2]{0:T(128)S(1)} %get-tuple-element.223.place_ref, bf16[8,2,256,2304]{3,2,1,0:T(8,128)(2,1)} %shard_map.273.q_ref.k_ref.v_ref, bf16[8,2,256,2304]{3,2,1,0:T(8,128)(2,1)} %shard_map.273.q_ref.k_ref.v_ref, ...), custom_call_target="tpu_custom_call" | custom-call | flops 28991029248 | bytes 10000000 | tf_op jit(solution)/shard_map/pallas_call | solution.py:592
  395.5 4.1 shard_map.283
  402.8 3.8 collective-permute-done.35
  410.8 11.5 %collective-permute-done.38 = bf16[4,80,768]{2,1,0:T(8,128)(2,1)S(1)} collective-permute-done((bf16[4,80,768]{2,1,0:T(8,128)(2,1)S(1)}, bf16[4,80,768]{2,1,0:T(8,128)(2,1)S(1)}, u32[]{:S(2)}, u32[]{:S(2)}) %collective-permute-start.38) | collective-permute-done | bytes 491552 | tf_op jit(solution)/shard_map/ppermute | solution.py:36
  422.4 9.7 %collective-permute-done.37 = bf16[4,80,768]{2,1,0:T(8,128)(2,1)S(1)} collective-permute-done((bf16[4,80,768]{2,1,0:T(8,128)(2,1)S(1)}, bf16[4,80,768]{2,1,0:T(8,128)(2,1)S(1)}, u32[]{:S(2)}, u32[]{:S(2)}) %collective-permute-start.37) | collective-permute-done | bytes 491552 | tf_op jit(solution)/shard_map/ppermute | solution.py:36
  432.4 4.3 collective-permute-start.41
  441.0 6.6 %collective-permute-done.40 = bf16[80,768]{1,0:T(8,128)(2,1)S(1)} collective-permute-done((bf16[80,768]{1,0:T(8,128)(2,1)S(1)}, bf16[80,768]{1,0:T(8,128)(2,1)S(1)}, u32[]{:S(2)}, u32[]{:S(2)}) %collective-permute-start.40) | collective-permute-done | bytes 122912 | tf_op jit(solution)/shard_map/ppermute | solution.py:41
  452.8 3.7 collective-permute-done.48.refs_3_
  460.4 5.5 %add_add_fusion.4 = f32[512,768]{1,0:T(8,128)} fusion(f32[512,768]{1,0:T(8,128)S(1)} %copy-done.37, bf16[768,2304]{1,0:T(8,128)(2,1)S(1)} %copy-done.2, bf16[512,768]{1,0:T(8,128)(2,1)S(1)} %get-tuple-element.199, bf16[512,768]{1,0:T(8,128)(2,1)S(1)} %copy-done.40, bf16[256,768]{1,0:T(8,128)(2,1)S(1)} %shard_map.280, bf16[256,768]{1,0:T(8,128)(2,1)S(1)} %shard_map.279, ...), kind=kOutput, calls=%fused_computation.65 | convolution fusion | flops 1822162944 | bytes 9046016 | tf_op jit(solution)/shard_map/rc,dc->rd/dot_general | solution.py:936
  (354 shorter events, 133.6 us)
Async XLA Ops:
  7.2 72.5 %all-gather.7.cloned.1.call-start = ((), (), s32[]{:S(2)}) async-start(), calls=%async_computation.1 | async-start | bytes 7077888 | tf_op jit(solution)/shard_map/all_gather | solution.py:774
  8.0 314.8 %all-gather.5.cloned.1.call-start = ((), (), s32[]{:S(2)}) async-start(), calls=%async_computation | async-start | bytes 7077888 | tf_op jit(solution)/shard_map/all_gather | solution.py:879
  14.3 37.8 %collective-permute-start.1 = (bf16[192,1152]{1,0:T(8,128)(2,1)S(1)}, bf16[192,1152]{1,0:T(8,128)(2,1)S(1)}, u32[]{:S(2)}, u32[]{:S(2)}) collective-permute-start(bf16[192,1152]{1,0:T(8,128)(2,1)S(1)} %constant_dynamic-slice_fusion.7), channel_id=1, source_target_pairs={{0,2},{1,3},{2,0},{3,1},{4,6},{5,7},{6,4},{7,5},{8,10},{9,11},{10,... | collective-permute-start | bytes 1327112 | tf_op jit(solution)/shard_map/ppermute | solution.py:41
  14.3 37.8 %collective-permute-start = (bf16[192,1152]{1,0:T(8,128)(2,1)S(1)}, bf16[192,1152]{1,0:T(8,128)(2,1)S(1)}, u32[]{:S(2)}, u32[]{:S(2)}) collective-permute-start(bf16[192,1152]{1,0:T(8,128)(2,1)S(1)} %constant_dynamic-slice_fusion.7), channel_id=1, source_target_pairs={{0,1},{1,2},{2,3},{3,0},{4,5},{5,6},{6,7},{7,4},{8,9},{9,10},{10,1... | collective-permute-start | bytes 1327112 | tf_op jit(solution)/shard_map/ppermute | solution.py:41
  75.0 25.7 %collective-permute-start.7 = (bf16[2,192,384]{2,1,0:T(8,128)(2,1)S(1)}, bf16[2,192,384]{2,1,0:T(8,128)(2,1)S(1)}, u32[]{:S(2)}, u32[]{:S(2)}) collective-permute-start(bf16[2,192,384]{2,1,0:T(8,128)(2,1)S(1)} %pad_maximum_fusion.11), channel_id=1, source_target_pairs={{0,1},{1,2},{2,3},{3,0},{4,5},{5,6},{6,7},{7,4},{8,9},{9,10},{10,1... | collective-permute-start | bytes 884744 | tf_op jit(solution)/shard_map/ppermute | solution.py:41
  75.1 25.6 %collective-permute-start.8 = (bf16[2,192,384]{2,1,0:T(8,128)(2,1)S(1)}, bf16[2,192,384]{2,1,0:T(8,128)(2,1)S(1)}, u32[]{:S(2)}, u32[]{:S(2)}) collective-permute-start(bf16[2,192,384]{2,1,0:T(8,128)(2,1)S(1)} %pad_maximum_fusion.11), channel_id=1, source_target_pairs={{0,2},{1,3},{2,0},{3,1},{4,6},{5,7},{6,4},{7,5},{8,10},{9,11},{10,... | collective-permute-start | bytes 884744 | tf_op jit(solution)/shard_map/ppermute | solution.py:41
  77.0 23.7 %collective-permute-start.9 = (bf16[2,192,384]{2,1,0:T(8,128)(2,1)S(1)}, bf16[2,192,384]{2,1,0:T(8,128)(2,1)S(1)}, u32[]{:S(2)}, u32[]{:S(2)}) collective-permute-start(bf16[2,192,384]{2,1,0:T(8,128)(2,1)S(1)} %pad_maximum_fusion.11), channel_id=1, source_target_pairs={{0,3},{1,0},{2,1},{3,2},{4,7},{5,4},{6,5},{7,6},{8,11},{9,8},{10,9... | collective-permute-start | bytes 884744 | tf_op jit(solution)/shard_map/ppermute | solution.py:41
  101.0 25.3 %collective-permute-start.10 = (bf16[3,192,384]{2,1,0:T(8,128)(2,1)S(1)}, bf16[3,192,384]{2,1,0:T(8,128)(2,1)S(1)}, u32[]{:S(2)}, u32[]{:S(2)}) collective-permute-start(bf16[3,192,384]{2,1,0:T(8,128)(2,1)S(1)} %get-tuple-element.94.refs_0_), channel_id=1, source_target_pairs={{0,8},{4,12},{8,0},{12,4},{16,24},{20,28},{24,16},{28,20},{1,9},{5... | collective-permute-start | bytes 1327112 | tf_op jit(solution)/shard_map/ppermute | solution.py:36
  102.5 23.8 %collective-permute-start.11 = (bf16[3,192,384]{2,1,0:T(8,128)(2,1)S(1)}, bf16[3,192,384]{2,1,0:T(8,128)(2,1)S(1)}, u32[]{:S(2)}, u32[]{:S(2)}) collective-permute-start(bf16[3,192,384]{2,1,0:T(8,128)(2,1)S(1)} %get-tuple-element.94.refs_0_), channel_id=1, source_target_pairs={{0,16},{4,20},{8,24},{12,28},{16,0},{20,4},{24,8},{28,12},{1,17},{... | collective-permute-start | bytes 1327112 | tf_op jit(solution)/shard_map/ppermute | solution.py:36
  104.0 22.3 %collective-permute-start.12 = (bf16[3,192,384]{2,1,0:T(8,128)(2,1)S(1)}, bf16[3,192,384]{2,1,0:T(8,128)(2,1)S(1)}, u32[]{:S(2)}, u32[]{:S(2)}) collective-permute-start(bf16[3,192,384]{2,1,0:T(8,128)(2,1)S(1)} %get-tuple-element.94.refs_0_), channel_id=1, source_target_pairs={{0,24},{4,28},{8,16},{12,20},{16,8},{20,12},{24,0},{28,4},{1,25},{... | collective-permute-start | bytes 1327112 | tf_op jit(solution)/shard_map/ppermute | solution.py:36
  131.8 24.1 %collective-permute-start.14 = (bf16[768,384]{1,0:T(8,128)(2,1)}, bf16[768,384]{1,0:T(8,128)(2,1)S(1)}, u32[]{:S(2)}, u32[]{:S(2)}) collective-permute-start(bf16[768,384]{1,0:T(8,128)(2,1)} %constant_dynamic-slice_fusion.6), channel_id=1, source_target_pairs={{0,1},{1,2},{2,3},{3,0},{4,5},{5,6},{6,7},{7,4},{8,9},{9,10},{10,1... | collective-permute-start | bytes 1769480 | tf_op jit(solution)/shard_map/ppermute | solution.py:41
  135.3 39.7 %collective-permute-start.15 = (bf16[768,384]{1,0:T(8,128)(2,1)}, bf16[768,384]{1,0:T(8,128)(2,1)S(1)}, u32[]{:S(2)}, u32[]{:S(2)}) collective-permute-start(bf16[768,384]{1,0:T(8,128)(2,1)} %constant_dynamic-slice_fusion.6), channel_id=1, source_target_pairs={{0,2},{1,3},{2,0},{3,1},{4,6},{5,7},{6,4},{7,5},{8,10},{9,11},{10,... | collective-permute-start | bytes 1769480 | tf_op jit(solution)/shard_map/ppermute | solution.py:41
  135.3 39.7 %collective-permute-start.16 = (bf16[768,384]{1,0:T(8,128)(2,1)}, bf16[768,384]{1,0:T(8,128)(2,1)S(1)}, u32[]{:S(2)}, u32[]{:S(2)}) collective-permute-start(bf16[768,384]{1,0:T(8,128)(2,1)} %constant_dynamic-slice_fusion.6), channel_id=1, source_target_pairs={{0,3},{1,0},{2,1},{3,2},{4,7},{5,4},{6,5},{7,6},{8,11},{9,8},{10,9... | collective-permute-start | bytes 1769480 | tf_op jit(solution)/shard_map/ppermute | solution.py:41
  175.2 21.9 %collective-permute-start.17 = (bf16[3,768,384]{2,1,0:T(8,128)(2,1)S(1)}, bf16[3,768,384]{2,1,0:T(8,128)(2,1)S(1)}, u32[]{:S(2)}, u32[]{:S(2)}) collective-permute-start(bf16[3,768,384]{2,1,0:T(8,128)(2,1)S(1)} %pad_maximum_fusion.5.refs_1_), channel_id=1, source_target_pairs={{0,4},{4,0},{8,12},{12,8},{16,20},{20,16},{24,28},{28,24},{1,5},{5... | collective-permute-start | bytes 5308424 | tf_op jit(solution)/shard_map/ppermute | solution.py:36
  239.7 31.3 %collective-permute-start.19 = (bf16[4,4,128,768]{3,2,1,0:T(8,128)(2,1)}, bf16[4,4,128,768]{3,2,1,0:T(8,128)(2,1)}, u32[]{:S(2)}, u32[]{:S(2)}) collective-permute-start(bf16[4,4,128,768]{3,2,1,0:T(8,128)(2,1)} %pad_maximum_fusion.2), channel_id=1, source_target_pairs={{0,4},{4,0},{8,12},{12,8},{16,20},{20,16},{24,28},{28,24},{1,5},{5... | collective-permute-start | bytes 9437192 | tf_op jit(solution)/shard_map/ppermute | solution.py:36
  245.2 43.7 %collective-permute-start.20 = (bf16[4,96,768]{2,1,0:T(8,128)(2,1)S(1)}, bf16[4,96,768]{2,1,0:T(8,128)(2,1)S(1)}, u32[]{:S(2)}, u32[]{:S(2)}) collective-permute-start(bf16[4,96,768]{2,1,0:T(8,128)(2,1)S(1)} %get-tuple-element.178), channel_id=1, source_target_pairs={{0,8},{4,12},{8,0},{12,4},{16,24},{20,28},{24,16},{28,20},{1,9},{5... | collective-permute-start | bytes 1769480 | tf_op jit(solution)/shard_map/ppermute | solution.py:36
  246.7 42.2 %collective-permute-start.21 = (bf16[4,96,768]{2,1,0:T(8,128)(2,1)S(1)}, bf16[4,96,768]{2,1,0:T(8,128)(2,1)S(1)}, u32[]{:S(2)}, u32[]{:S(2)}) collective-permute-start(bf16[4,96,768]{2,1,0:T(8,128)(2,1)S(1)} %get-tuple-element.177), channel_id=1, source_target_pairs={{0,16},{4,20},{8,24},{12,28},{16,0},{20,4},{24,8},{28,12},{1,17},{... | collective-permute-start | bytes 1769480 | tf_op jit(solution)/shard_map/ppermute | solution.py:36
  248.2 43.8 %collective-permute-start.22 = (bf16[4,96,768]{2,1,0:T(8,128)(2,1)S(1)}, bf16[4,96,768]{2,1,0:T(8,128)(2,1)S(1)}, u32[]{:S(2)}, u32[]{:S(2)}) collective-permute-start(bf16[4,96,768]{2,1,0:T(8,128)(2,1)S(1)} %get-tuple-element.176), channel_id=1, source_target_pairs={{0,24},{4,28},{8,16},{12,20},{16,8},{20,12},{24,0},{28,4},{1,25},{... | collective-permute-start | bytes 1769480 | tf_op jit(solution)/shard_map/ppermute | solution.py:36
  293.1 29.6 %collective-permute-start.26 = (bf16[96,768]{1,0:T(8,128)(2,1)}, bf16[96,768]{1,0:T(8,128)(2,1)}, u32[]{:S(2)}, u32[]{:S(2)}) collective-permute-start(bf16[96,768]{1,0:T(8,128)(2,1)} %get-tuple-element.194), channel_id=1, source_target_pairs={{0,1},{1,2},{2,3},{3,0},{4,5},{5,6},{6,7},{7,4},{8,9},{9,10},{10,1... | collective-permute-start | bytes 442376 | tf_op jit(solution)/shard_map/ppermute | solution.py:41
  312.1 39.8 %collective-permute-start.23 = (bf16[4,128,768]{2,1,0:T(8,128)(2,1)}, bf16[4,128,768]{2,1,0:T(8,128)(2,1)S(1)}, u32[]{:S(2)}, u32[]{:S(2)}) collective-permute-start(bf16[4,128,768]{2,1,0:T(8,128)(2,1)} %get-tuple-element.175), channel_id=1, source_target_pairs={{0,8},{4,12},{8,0},{12,4},{16,24},{20,28},{24,16},{28,20},{1,9},{5... | collective-permute-start | bytes 2359304 | tf_op jit(solution)/shard_map/ppermute | solution.py:36
  313.6 38.7 %collective-permute-start.24 = (bf16[4,128,768]{2,1,0:T(8,128)(2,1)}, bf16[4,128,768]{2,1,0:T(8,128)(2,1)}, u32[]{:S(2)}, u32[]{:S(2)}) collective-permute-start(bf16[4,128,768]{2,1,0:T(8,128)(2,1)} %get-tuple-element.174), channel_id=1, source_target_pairs={{0,16},{4,20},{8,24},{12,28},{16,0},{20,4},{24,8},{28,12},{1,17},{... | collective-permute-start | bytes 2359304 | tf_op jit(solution)/shard_map/ppermute | solution.py:36
  314.2 38.2 %collective-permute-start.25 = (bf16[4,128,768]{2,1,0:T(8,128)(2,1)}, bf16[4,128,768]{2,1,0:T(8,128)(2,1)}, u32[]{:S(2)}, u32[]{:S(2)}) collective-permute-start(bf16[4,128,768]{2,1,0:T(8,128)(2,1)} %get-tuple-element.173), channel_id=1, source_target_pairs={{0,24},{4,28},{8,16},{12,20},{16,8},{20,12},{24,0},{28,4},{1,25},{... | collective-permute-start | bytes 2359304 | tf_op jit(solution)/shard_map/ppermute | solution.py:36
  315.7 31.9 %collective-permute-start.27 = (bf16[96,768]{1,0:T(8,128)(2,1)}, bf16[96,768]{1,0:T(8,128)(2,1)}, u32[]{:S(2)}, u32[]{:S(2)}) collective-permute-start(bf16[96,768]{1,0:T(8,128)(2,1)} %get-tuple-element.193), channel_id=1, source_target_pairs={{0,2},{1,3},{2,0},{3,1},{4,6},{5,7},{6,4},{7,5},{8,10},{9,11},{10,... | collective-permute-start | bytes 442376 | tf_op jit(solution)/shard_map/ppermute | solution.py:41
  322.7 24.9 %collective-permute-start.28 = (bf16[96,768]{1,0:T(8,128)(2,1)}, bf16[96,768]{1,0:T(8,128)(2,1)}, u32[]{:S(2)}, u32[]{:S(2)}) collective-permute-start(bf16[96,768]{1,0:T(8,128)(2,1)} %get-tuple-element.192), channel_id=1, source_target_pairs={{0,3},{1,0},{2,1},{3,2},{4,7},{5,4},{6,5},{7,6},{8,11},{9,8},{10,9... | collective-permute-start | bytes 442376 | tf_op jit(solution)/shard_map/ppermute | solution.py:41
  348.8 38.5 %collective-permute-start.34 = (bf16[96,768]{1,0:T(8,128)(2,1)S(1)}, bf16[96,768]{1,0:T(8,128)(2,1)S(1)}, u32[]{:S(2)}, u32[]{:S(2)}) collective-permute-start(bf16[96,768]{1,0:T(8,128)(2,1)S(1)} %fusion.43.refs_0_), channel_id=1, source_target_pairs={{0,24},{4,28},{8,16},{12,20},{16,8},{20,12},{24,0},{28,4},{1,25},{... | collective-permute-start | bytes 442376 | tf_op jit(solution)/shard_map/ppermute | solution.py:36
  350.3 40.0 %collective-permute-start.33 = (bf16[96,768]{1,0:T(8,128)(2,1)S(1)}, bf16[96,768]{1,0:T(8,128)(2,1)S(1)}, u32[]{:S(2)}, u32[]{:S(2)}) collective-permute-start(bf16[96,768]{1,0:T(8,128)(2,1)S(1)} %fusion.43.refs_0_), channel_id=1, source_target_pairs={{0,16},{4,20},{8,24},{12,28},{16,0},{20,4},{24,8},{28,12},{1,17},{... | collective-permute-start | bytes 442376 | tf_op jit(solution)/shard_map/ppermute | solution.py:36
  351.8 38.4 %collective-permute-start.32 = (bf16[96,768]{1,0:T(8,128)(2,1)S(1)}, bf16[96,768]{1,0:T(8,128)(2,1)S(1)}, u32[]{:S(2)}, u32[]{:S(2)}) collective-permute-start(bf16[96,768]{1,0:T(8,128)(2,1)S(1)} %fusion.43.refs_0_), channel_id=1, source_target_pairs={{0,8},{4,12},{8,0},{12,4},{16,24},{20,28},{24,16},{28,20},{1,9},{5... | collective-permute-start | bytes 442376 | tf_op jit(solution)/shard_map/ppermute | solution.py:36
  354.4 36.9 %collective-permute-start.29 = (bf16[128,768]{1,0:T(8,128)(2,1)S(1)}, bf16[128,768]{1,0:T(8,128)(2,1)S(1)}, u32[]{:S(2)}, u32[]{:S(2)}) collective-permute-start(bf16[128,768]{1,0:T(8,128)(2,1)S(1)} %get-tuple-element.189), channel_id=1, source_target_pairs={{0,1},{1,2},{2,3},{3,0},{4,5},{5,6},{6,7},{7,4},{8,9},{9,10},{10,1... | collective-permute-start | bytes 589832 | tf_op jit(solution)/shard_map/ppermute | solution.py:41
  356.4 34.8 %collective-permute-start.30 = (bf16[128,768]{1,0:T(8,128)(2,1)S(1)}, bf16[128,768]{1,0:T(8,128)(2,1)S(1)}, u32[]{:S(2)}, u32[]{:S(2)}) collective-permute-start(bf16[128,768]{1,0:T(8,128)(2,1)S(1)} %get-tuple-element.188), channel_id=1, source_target_pairs={{0,2},{1,3},{2,0},{3,1},{4,6},{5,7},{6,4},{7,5},{8,10},{9,11},{10,... | collective-permute-start | bytes 589832 | tf_op jit(solution)/shard_map/ppermute | solution.py:41
  408.8 23.2 %collective-permute-start.37 = (bf16[4,80,768]{2,1,0:T(8,128)(2,1)S(1)}, bf16[4,80,768]{2,1,0:T(8,128)(2,1)S(1)}, u32[]{:S(2)}, u32[]{:S(2)}) collective-permute-start(bf16[4,80,768]{2,1,0:T(8,128)(2,1)S(1)} %get-tuple-element.181), channel_id=1, source_target_pairs={{0,16},{4,20},{8,24},{12,28},{16,0},{20,4},{24,8},{28,12},{1,17},{... | collective-permute-start | bytes 1474568 | tf_op jit(solution)/shard_map/ppermute | solution.py:36
  409.3 22.7 %collective-permute-start.36 = (bf16[4,80,768]{2,1,0:T(8,128)(2,1)S(1)}, bf16[4,80,768]{2,1,0:T(8,128)(2,1)S(1)}, u32[]{:S(2)}, u32[]{:S(2)}) collective-permute-start(bf16[4,80,768]{2,1,0:T(8,128)(2,1)S(1)} %get-tuple-element.179), channel_id=1, source_target_pairs={{0,8},{4,12},{8,0},{12,4},{16,24},{20,28},{24,16},{28,20},{1,9},{5... | collective-permute-start | bytes 1474568 | tf_op jit(solution)/shard_map/ppermute | solution.py:36
  437.4 28.6 %collective-permute-start.50 = (bf16[4,96,768]{2,1,0:T(8,128)(2,1)S(1)}, bf16[4,96,768]{2,1,0:T(8,128)(2,1)S(1)}, u32[]{:S(2)}, u32[]{:S(2)}) collective-permute-start(bf16[4,96,768]{2,1,0:T(8,128)(2,1)S(1)} %copy-done.43), channel_id=1, source_target_pairs={{0,4},{4,0},{8,12},{12,8},{16,20},{20,16},{24,28},{28,24},{1,5},{5... | collective-permute-start | bytes 1769480 | tf_op jit(solution)/shard_map/ppermute | solution.py:36
  (81 other events, 1125.7 us)
Sparse Core Ops, SparseCore 0:
  10.0 48.2 all-gather.6
  228.1 73.7 all-gather.4
